TPU v7x, 32 devices: a whole 2x2x4 slice. The times are simulated.
32 devices in a mesh: leaf: 8 (over y, x, core), row: 4 (over z).
Axes of the slice: x: 2, y: 2, z: 4, core: 2. Of those that a mesh axis runs over, the one named last changes fastest.
Arguments:
- rhs: bfloat16 [8, 4, 720, 512], P('leaf', 'row'), may hold values from -6 to 6
- inv_diag: bfloat16 [8, 4, 720, 1536], P('leaf', 'row'), may hold values from -0.15625 to 0.15625
- off_diag: bfloat16 [8, 4, 384, 6528], P('leaf', 'row'), may hold values from -0.078125 to 0.078125
- pair_mask: int32 [8, 4, 6], P('leaf', 'row'), may hold values 0 or 1
Outputs:
- solution: float32 [8, 4, 720, 512], P('leaf', 'row')
All inputs are finite; a program needn't handle non-finite values. No bound on the sum of `pair_mask` on one device may be relied on, other than what follows from the above.
Results may differ from a plain program's by a relative error of at most 0.0065.
Values may be sent and summed in bfloat16 or wider, within the bound.
A program may use at most 64 MiB of HBM per device.

v0:
```python
import jax
import jax.numpy as jnp
from jax import lax
from jax.sharding import PartitionSpec as P


def partner_2(block, axis, bit):
    count = lax.axis_size(axis)
    route = []
    for low in range(count):
        high = low | 1 << bit
        if high != low and high < count:
            route += [(low, high), (high, low)]
    return lax.ppermute(block, axis, route)


def column_start(ancestor, width_all):
    offset = 0
    for higher in range(1, ancestor):
        for within in range(higher):
            offset += width_all // 2**within
    return offset


def shards(rhs, inv_diag, off_diag, pair_mask):
    rows_n = lax.axis_size("row")
    leaves = lax.axis_size("leaf")
    levels_n = leaves.bit_length() - 1
    leaf_index = lax.axis_index("leaf")
    width_all = inv_diag.shape[3]
    right_all = rhs[0, 0]
    inverse_all = inv_diag[0, 0]
    panels = off_diag[0, 0]
    live_pairs = pair_mask[0, 0].astype(jnp.bfloat16)
    known_parts = []
    outputs = []
    offset = 0
    for ancestor in range(levels_n + 1):
        height = width_all // (2**ancestor * rows_n)
        own_rhs = right_all[offset : offset + height]
        own_inv = inverse_all[offset : offset + height]
        offset += height
        if ancestor > 0:
            stacked = jnp.concatenate(
                [
                    known_parts[source] * live_pairs[ancestor * (ancestor - 1) // 2 + source]
                    for source in range(ancestor)
                ],
                axis=0,
            )
            first_col = column_start(ancestor, width_all)
            span_cols = stacked.shape[0]
            update = jnp.dot(
                panels[:, first_col : first_col + span_cols],
                stacked,
                preferred_element_type=jnp.float32,
            )
        if ancestor > 0:
            current = update
            for bit_pos in reversed(range(ancestor)):
                half_rows = current.shape[0] // 2
                upper_half = leaf_index // 2**bit_pos % 2 == 1
                kept_rows = jnp.where(upper_half, current[half_rows:], current[:half_rows])
                sent_rows = jnp.where(upper_half, current[:half_rows], current[half_rows:])
                current = kept_rows + partner_2(
                    sent_rows.astype(jnp.bfloat16), "leaf", bit_pos
                ).astype(sent_rows.dtype)
            reduced = (own_rhs.astype(jnp.float32) - current).astype(jnp.bfloat16)
        else:
            reduced = own_rhs
        gathered = lax.all_gather(reduced, "row", axis=0, tiled=True)
        for bit_pos in range(ancestor):
            partner = partner_2(gathered, "leaf", bit_pos)
            upper_half = leaf_index // 2**bit_pos % 2 == 1
            gathered = jnp.where(
                upper_half,
                jnp.concatenate([partner, gathered], axis=0),
                jnp.concatenate([gathered, partner], axis=0),
            )
        solved = jnp.dot(own_inv, gathered, preferred_element_type=jnp.float32)
        outputs.append(solved)
        if ancestor < levels_n:
            leaf_part = lax.all_gather(solved.astype(jnp.bfloat16), "row", axis=0, tiled=True)
            known_parts.append(leaf_part)
    return jnp.concatenate(outputs, axis=0)[None, None]


def solution(mesh):
    in_specs = (
        P("leaf", "row", None, None),
        P("leaf", "row", None, None),
        P("leaf", "row", None, None),
        P("leaf", "row", None),
    )
    out_specs = P("leaf", "row", None, None)
    return jax.shard_map(shards, mesh=mesh, in_specs=in_specs, out_specs=out_specs, check_vma=False)
```

profile of v0, /device:TPU:0, one launch (start us, length us, event | category | flops | bytes accessed | tf_op | source)
XLA Modules:
  0.0 272.4 jit_solution(6120257466806797405)
XLA Ops:
  6.5 1.8 slice.125
  8.4 40.4 %all-gather.6.cloned.1.call-done = bf16[1,1,1536,512]{3,2,1,0:T(8,128)(2,1)} async-done(((bf16[1,1,384,512]{3,2,1,0:T(8,128)(2,1)}), bf16[1,1,1536,512]{3,2,1,0:T(8,128)(2,1)}) %all-gather.6.cloned.1.call-update) | async-done | bytes 1572880 | tf_op jit(solution)/shard_map/all_gather | solution.py:71
  48.8 3.6 %fusion.72 = (bf16[384,512]{1,0:T(8,128)(2,1)}, f32[384,512]{1,0:T(8,128)}) fusion(bf16[1,1,1536,512]{3,2,1,0:T(8,128)(2,1)} %all-gather.6.cloned.1.call-done, bf16[1,1,720,1536]{3,2,1,0:T(8,128)(2,1)} %param.5), kind=kOutput, calls=%fused_computation.86 | convolution fusion | flops 604176384 | bytes 3932160 | tf_op jit(solution)/shard_map/dot_general | solution.py:80
  53.1 35.4 %all-gather.4.cloned.1.call-done = bf16[1536,512]{1,0:T(8,128)(2,1)} async-done(((bf16[384,512]{1,0:T(8,128)(2,1)}), bf16[1536,512]{1,0:T(8,128)(2,1)}) %all-gather.4.cloned.1.call-update) | async-done | bytes 1572880 | tf_op jit(solution)/shard_map/all_gather | solution.py:83
  88.5 3.1 %fusion.47 = f32[384,512]{1,0:T(8,128)S(1)} fusion(bf16[1536,512]{1,0:T(8,128)(2,1)} %all-gather.4.cloned.1.call-done, bf16[384,6528]{1,0:T(8,128)(2,1)} %bitcast.53, bf16[]{:T(256)} %bitcast.3), kind=kOutput, calls=%fused_computation.43 | convolution fusion | flops 604766208 | bytes 3539456 | tf_op jit(solution)/shard_map/dot_general | solution.py:53
  91.7 1.4 collective-permute-done
  94.2 18.3 %all_gather.23 = bf16[768,512]{1,0:T(8,128)(2,1)} all-gather(bf16[192,512]{1,0:T(8,128)(2,1)S(1)} %fusion.59), channel_id=1, replica_groups=mesh['leaf'=8,'row'=4] {'row'}, dimensions={0}, use_global_device_ids=true | all-gather | bytes 983040 | tf_op jit(solution)/shard_map/all_gather | solution.py:71
  112.5 1.5 broadcast_multiply_fusion
  115.1 2.6 fusion.73
  117.7 18.1 %all_gather.24 = bf16[768,512]{1,0:T(8,128)(2,1)S(1)} all-gather(bf16[192,512]{1,0:T(8,128)(2,1)S(1)} %get-tuple-element.17), channel_id=1, replica_groups=mesh['leaf'=8,'row'=4] {'row'}, dimensions={0}, use_global_device_ids=true | all-gather | bytes 983040 | tf_op jit(solution)/shard_map/all_gather | solution.py:83
  135.8 1.3 broadcast_multiply_fusion.2
  137.2 2.5 fusion.37
  139.8 1.6 collective-permute-start.2
  141.3 4.2 %collective-permute-done.2 = bf16[192,512]{1,0:T(8,128)(2,1)S(1)} collective-permute-done((bf16[192,512]{1,0:T(8,128)(2,1)S(1)}, bf16[192,512]{1,0:T(8,128)(2,1)S(1)}, u32[]{:S(2)}, u32[]{:S(2)}) %collective-permute-start.2) | collective-permute-done | bytes 196640 | tf_op jit(solution)/shard_map/ppermute | solution.py:14
  147.9 14.5 %all_gather.25 = bf16[384,512]{1,0:T(8,128)(2,1)S(1)} all-gather(bf16[96,512]{1,0:T(8,128)(2,1)S(1)} %fusion.62), channel_id=1, replica_groups=mesh['leaf'=8,'row'=4] {'row'}, dimensions={0}, use_global_device_ids=true | all-gather | bytes 491520 | tf_op jit(solution)/shard_map/all_gather | solution.py:71
  162.4 1.7 collective-permute-done.4
  164.5 1.8 collective-permute-start.5
  166.3 18.0 %collective-permute-done.5 = bf16[768,512]{1,0:T(8,128)(2,1)} collective-permute-done((bf16[768,512]{1,0:T(8,128)(2,1)S(1)}, bf16[768,512]{1,0:T(8,128)(2,1)}, u32[]{:S(2)}, u32[]{:S(2)}) %collective-permute-start.5) | collective-permute-done | bytes 786464 | tf_op jit(solution)/shard_map/ppermute | solution.py:14
  184.2 2.0 fusion.74
  186.3 14.4 %all_gather.26 = bf16[384,512]{1,0:T(8,128)(2,1)S(1)} all-gather(bf16[96,512]{1,0:T(8,128)(2,1)S(1)} %get-tuple-element.19), channel_id=1, replica_groups=mesh['leaf'=8,'row'=4] {'row'}, dimensions={0}, use_global_device_ids=true | all-gather | bytes 491520 | tf_op jit(solution)/shard_map/all_gather | solution.py:83
  201.3 2.9 %fusion.42 = f32[384,512]{1,0:T(8,128)S(1)} fusion(bf16[384,512]{1,0:T(8,128)(2,1)S(1)} %broadcast_multiply_fusion.4, bf16[768,512]{1,0:T(8,128)(2,1)S(1)} %get-tuple-element.7, bf16[1536,512]{1,0:T(8,128)(2,1)S(1)} %get-tuple-element.5, bf16[384,6528]{1,0:T(8,128)(2,1)} %bitcast.55), kind=kOutput, calls=%fused_computation.42 | convolution fusion | flops 1065222144 | bytes 5603328 | tf_op jit(solution)/shard_map/dot_general | solution.py:53
  204.2 2.0 collective-permute-start.6
  206.2 3.7 %collective-permute-done.6 = bf16[192,512]{1,0:T(8,128)(2,1)S(1)} collective-permute-done((bf16[192,512]{1,0:T(8,128)(2,1)S(1)}, bf16[192,512]{1,0:T(8,128)(2,1)S(1)}, u32[]{:S(2)}, u32[]{:S(2)}) %collective-permute-start.6) | collective-permute-done | bytes 196640 | tf_op jit(solution)/shard_map/ppermute | solution.py:14
  210.1 2.0 collective-permute-start.7
  212.1 2.7 collective-permute-done.7
  216.9 13.7 %all_gather.27 = bf16[192,512]{1,0:T(8,128)(2,1)S(1)} all-gather(bf16[48,512]{1,0:T(8,128)(2,1)S(1)} %fusion.65), channel_id=1, replica_groups=mesh['leaf'=8,'row'=4] {'row'}, dimensions={0}, use_global_device_ids=true | all-gather | bytes 245760 | tf_op jit(solution)/shard_map/all_gather | solution.py:71
  230.6 1.4 collective-permute-done.9
  232.2 1.9 collective-permute-start.10
  234.1 9.4 %collective-permute-done.10 = bf16[384,512]{1,0:T(8,128)(2,1)S(1)} collective-permute-done((bf16[384,512]{1,0:T(8,128)(2,1)S(1)}, bf16[384,512]{1,0:T(8,128)(2,1)S(1)}, u32[]{:S(2)}, u32[]{:S(2)}) %collective-permute-start.10) | collective-permute-done | bytes 393248 | tf_op jit(solution)/shard_map/ppermute | solution.py:14
  243.8 1.8 collective-permute-start.11
  245.7 17.1 %collective-permute-done.11 = bf16[768,512]{1,0:T(8,128)(2,1)S(1)} collective-permute-done((bf16[768,512]{1,0:T(8,128)(2,1)S(1)}, bf16[768,512]{1,0:T(8,128)(2,1)S(1)}, u32[]{:S(2)}, u32[]{:S(2)}) %collective-permute-start.11) | collective-permute-done | bytes 786464 | tf_op jit(solution)/shard_map/ppermute | solution.py:14
  262.7 1.6 fusion.55
  (38 shorter events, 10.5 us)
Async XLA Ops:
  6.5 42.2 %all-gather.6.cloned.1.call-start = ((), (), s32[]{:S(2)}) async-start(), calls=%async_computation.1 | async-start | bytes 1966080 | tf_op jit(solution)/shard_map/all_gather | solution.py:71
  8.3 44.0 %copy-start.2 = (s32[1,1,6]{2,1,0:T(1,128)S(1)}, s32[1,1,6]{2,1,0:T(1,128)}, u32[]{:S(2)}) copy-start(s32[1,1,6]{2,1,0:T(1,128)} %param.7) | copy-start | bytes 76
  8.3 80.1 %all-gather.4.cloned.1.call-start = ((), (), s32[]{:S(2)}) async-start(), calls=%async_computation | async-start | bytes 1966080 | tf_op jit(solution)/shard_map/all_gather | solution.py:83
  91.6 20.9 %copy-start = (bf16[1536,512]{1,0:T(8,128)(2,1)S(1)}, bf16[1536,512]{1,0:T(8,128)(2,1)}, u32[]{:S(2)}) copy-start(bf16[1536,512]{1,0:T(8,128)(2,1)} %all-gather.4.cloned.1.call-done) | copy-start | bytes 4718596
  91.6 1.5 collective-permute-start
  112.5 2.6 collective-permute-start.1
  139.8 5.7 %collective-permute-start.2 = (bf16[192,512]{1,0:T(8,128)(2,1)S(1)}, bf16[192,512]{1,0:T(8,128)(2,1)S(1)}, u32[]{:S(2)}, u32[]{:S(2)}) collective-permute-start(bf16[192,512]{1,0:T(8,128)(2,1)S(1)} %select_convert_fusion.1), channel_id=1, source_target_pairs={{0,8},{8,0},{4,12},{12,4},{16,24},{24,16},{20,28},{28,20},{1,9},{9... | collective-permute-start | bytes 589832 | tf_op jit(solution)/shard_map/ppermute | solution.py:14
  145.6 1.4 collective-permute-start.3
  162.4 1.7 collective-permute-start.4
  164.5 19.8 %collective-permute-start.5 = (bf16[768,512]{1,0:T(8,128)(2,1)S(1)}, bf16[768,512]{1,0:T(8,128)(2,1)}, u32[]{:S(2)}, u32[]{:S(2)}) collective-permute-start(bf16[768,512]{1,0:T(8,128)(2,1)S(1)} %maximum_select_fusion.12), channel_id=1, source_target_pairs={{0,8},{8,0},{4,12},{12,4},{16,24},{24,16},{20,28},{28,20},{1,9},{9... | collective-permute-start | bytes 2359304 | tf_op jit(solution)/shard_map/ppermute | solution.py:14
  204.2 5.7 %collective-permute-start.6 = (bf16[192,512]{1,0:T(8,128)(2,1)S(1)}, bf16[192,512]{1,0:T(8,128)(2,1)S(1)}, u32[]{:S(2)}, u32[]{:S(2)}) collective-permute-start(bf16[192,512]{1,0:T(8,128)(2,1)S(1)} %select_convert_fusion), channel_id=1, source_target_pairs={{0,16},{16,0},{4,20},{20,4},{8,24},{24,8},{12,28},{28,12},{1,17},{... | collective-permute-start | bytes 589832 | tf_op jit(solution)/shard_map/ppermute | solution.py:14
  210.1 4.7 %collective-permute-start.7 = (bf16[96,512]{1,0:T(8,128)(2,1)S(1)}, bf16[96,512]{1,0:T(8,128)(2,1)S(1)}, u32[]{:S(2)}, u32[]{:S(2)}) collective-permute-start(bf16[96,512]{1,0:T(8,128)(2,1)S(1)} %select_convert_fusion.3), channel_id=1, source_target_pairs={{0,8},{8,0},{4,12},{12,4},{16,24},{24,16},{20,28},{28,20},{1,9},{9... | collective-permute-start | bytes 294920 | tf_op jit(solution)/shard_map/ppermute | solution.py:14
  214.8 1.3 collective-permute-start.8
  230.6 1.4 collective-permute-start.9
  232.2 11.3 %collective-permute-start.10 = (bf16[384,512]{1,0:T(8,128)(2,1)S(1)}, bf16[384,512]{1,0:T(8,128)(2,1)S(1)}, u32[]{:S(2)}, u32[]{:S(2)}) collective-permute-start(bf16[384,512]{1,0:T(8,128)(2,1)S(1)} %maximum_select_fusion.14), channel_id=1, source_target_pairs={{0,8},{8,0},{4,12},{12,4},{16,24},{24,16},{20,28},{28,20},{1,9},{9... | collective-permute-start | bytes 1179656 | tf_op jit(solution)/shard_map/ppermute | solution.py:14
  243.8 20.5 %copy-start.1 = (f32[384,512]{1,0:T(8,128)S(1)}, f32[384,512]{1,0:T(8,128)}, u32[]{:S(2)}) copy-start(f32[384,512]{1,0:T(8,128)} %get-tuple-element.16) | copy-start | bytes 2359300
  243.8 18.9 %collective-permute-start.11 = (bf16[768,512]{1,0:T(8,128)(2,1)S(1)}, bf16[768,512]{1,0:T(8,128)(2,1)S(1)}, u32[]{:S(2)}, u32[]{:S(2)}) collective-permute-start(bf16[768,512]{1,0:T(8,128)(2,1)S(1)} %maximum_select_fusion.13), channel_id=1, source_target_pairs={{0,16},{16,0},{4,20},{20,4},{8,24},{24,8},{12,28},{28,12},{1,17},{... | collective-permute-start | bytes 2359304 | tf_op jit(solution)/shard_map/ppermute | solution.py:14
Sparse Core Ops, SparseCore 0:
  8.9 39.7 all-gather.5
  52.5 35.9 all-gather.3
where the time goes:
time: 273 us; the launch traced here: 272 us
  waiting for transfers between devices  139 us (51%)
  blocking collectives  78.9 us (29%)
  matrix products  18.3 us (7%)
  between operations  13.7 us (5%)
  starting transfers between devices  11.3 us (4%)
  other arithmetic  8.65 us (3%)
    ppermute x12, waiting for transfers between devices, partner_2(): return lax.ppermute(block, axis, route)  63.3 us
    all_gather x3, blocking collectives, shards(): gathered = lax.all_gather(reduced, 'row', axis=0, tiled=True)  46.5 us
    all_gather x1, waiting for transfers between devices, shards(): gathered = lax.all_gather(reduced, 'row', axis=0, tiled=True)  40.4 us
    all_gather x1, waiting for transfers between devices, shards(): lax.all_gather(solved.astype(jnp.bfloat16), 'row', axis=0, tiled=True)  35.4 us
    all_gather x2, blocking collectives, shards(): lax.all_gather(solved.astype(jnp.bfloat16), 'row', axis=0, tiled=True)  32.5 us
    ppermute x12, starting transfers between devices, partner_2(): return lax.ppermute(block, axis, route)  11.3 us
    dot_general x4, matrix products, shards(): solved = jnp.dot(own_inv, gathered, preferred_element_type=jnp.float32)  9.82 us
    dot_general x3, matrix products, shards(): jnp.dot(panels[:, first_col:first_col + span_cols], stacked, preferred_el...  8.51 us
  transfers between devices with their start and end apart: 14, of which 14 were waited for; matrix products, arithmetic and copies ran while one was open for 1% of the time, Pallas kernels for 0%

commit v1 on v0

--- a/solution.py
+++ b/solution.py
@@ -1,7 +1,17 @@
+import functools
+
 import jax
 import jax.numpy as jnp
 from jax import lax
+from jax.experimental import pallas as pl
+from jax.experimental.pallas import tpu as pltpu
 from jax.sharding import PartitionSpec as P
+
+LANES = 128
+ROW_TILE = 16
+CHUNKS = 2
+TREE_LEVELS = 3
+MESH = pl.DeviceIdType.MESH
 
 
 def partner_2(block, axis, bit):
@@ -85,6 +95,417 @@
     return jnp.concatenate(outputs, axis=0)[None, None]
 
 
+def dot32(left, right):
+    return jnp.dot(left, right, preferred_element_type=jnp.float32)
+
+
+GATHERS = ["z0a", "z0b", "y0a", "y0b", "z1a", "z1b", "y1a", "y1b", "z2", "y2", "z3"]
+SWAPS = ["b1a", "b1b", "b2", "b3", "d1", "d2", "d3", "u1a", "u1b", "u2", "u3", "y1a", "y1b", "y2", "y3"]
+LOCALS = ["z0a", "z0b", "d0", "p1", "p2", "p3", "d1", "d2", "d3", "b1a", "b1b", "b2", "b3"]
+
+
+def tree_kernel(
+    rows_n, leaves_n,
+    mask, rhs, inv, pan, out,
+    d0, d1, d2, d3, p1, p2, p3, b1, b2, b3,
+    z0, z1, z2, z3, y0, y1, y2,
+    u1, u2, u3, u1s, u2s, u3s, u1r, u2r, u3r, y1s, y2s, y3s, y3r,
+    up_sem, down_sem, land_sem, swap_send, swap_recv, local_sem,
+):
+    leaf = lax.axis_index("leaf")
+    row = lax.axis_index("row")
+    height = p1.shape[0]
+    right_n = u2.shape[1]
+    chunk = right_n // CHUNKS
+    heights = [height // 2**m for m in range(TREE_LEVELS + 1)]
+    starts = [sum(heights[:m]) for m in range(TREE_LEVELS + 1)]
+    wide = LANES
+    suffix = "ab"
+    pending = []
+    place = [leaf % 2**m for m in range(TREE_LEVELS + 1)]
+
+    def at_cols(index):
+        return pl.ds(pl.multiple_of(index * wide, wide), wide)
+
+    def level_rows(m):
+        return pl.ds(starts[m], heights[m])
+
+    barrier = pltpu.get_barrier_semaphore()
+
+    @pl.when(row < rows_n - 1)
+    def _():
+        pl.semaphore_signal(barrier, inc=1, device_id=(leaf, row + 1), device_id_type=MESH)
+
+    @pl.when(row > 0)
+    def _():
+        pl.semaphore_signal(barrier, inc=1, device_id=(leaf, row - 1), device_id_type=MESH)
+
+    for d in range(1, leaves_n):
+        pl.semaphore_signal(barrier, inc=1, device_id=((leaf + d) % leaves_n, row), device_id_type=MESH)
+
+    def local(name, src, dst):
+        return pltpu.make_async_copy(src, dst, local_sem.at[LOCALS.index(name)])
+
+    local_copies = {}
+    for c in range(CHUNKS):
+        local_copies["z0" + suffix[c]] = local(
+            "z0" + suffix[c], rhs.at[pl.ds(0, height), pl.ds(c * chunk, chunk)], z0.at[c, row])
+    local_copies["d0"] = local("d0", inv.at[pl.ds(0, height)], d0)
+    for m, held in ((1, p1), (2, p2), (3, p3)):
+        local_copies["p%d" % m] = local(
+            "p%d" % m, pan.at[:, pl.ds(column_start(m, d0.shape[1]), held.shape[1])], held)
+    for m, held in ((1, d1), (2, d2), (3, d3)):
+        local_copies["d%d" % m] = local("d%d" % m, inv.at[level_rows(m)], held.at[place[m]])
+    for c in range(CHUNKS):
+        local_copies["b1" + suffix[c]] = local(
+            "b1" + suffix[c], rhs.at[level_rows(1), at_cols(2 * c + place[1])], b1.at[c, place[1]])
+    local_copies["b2"] = local("b2", rhs.at[level_rows(2), at_cols(place[2])], b2.at[place[2]])
+    local_copies["b3"] = local("b3", rhs.at[level_rows(3), at_cols(place[3] // 2)], b3.at[place[3]])
+    for name in LOCALS:
+        local_copies[name].start()
+
+    def hops():
+        return jnp.where(row > 0, 1, 0) + jnp.where(row < rows_n - 1, 1, 0)
+
+    pl.semaphore_wait(barrier, hops() + leaves_n - 1)
+
+    def hop(name, src, dst, step, source, way):
+        k = GATHERS.index(name)
+        sem = up_sem if way > 0 else down_sem
+        return pltpu.make_async_remote_copy(
+            src_ref=src, dst_ref=dst, send_sem=sem.at[k, step], recv_sem=land_sem.at[k, source],
+            device_id=(leaf, row + way), device_id_type=MESH)
+
+    def gather_start(name, slot, src=None):
+        for way, can in ((1, row < rows_n - 1), (-1, row > 0)):
+            def make(way=way):
+                return hop(name, slot(row) if src is None else src, slot(row), 0, row, way)
+
+            @pl.when(can)
+            def _(make=make):
+                make().start()
+
+            pending.append((can, make))
+
+    def gather_step(name, slot, step):
+        for way, can in ((1, row < rows_n - 1), (-1, row > 0)):
+            source = row - way * step
+            there = (source >= 0) if way > 0 else (source < rows_n)
+
+            def make(way=way, source=source):
+                return hop(name, slot(source), slot(source), step, source, way)
+
+            @pl.when(there)
+            def _(make=make):
+                make().wait_recv()
+
+            if step < rows_n - 1:
+                both = jnp.logical_and(there, can)
+
+                @pl.when(both)
+                def _(make=make):
+                    make().start()
+
+                pending.append((both, make))
+
+    def peer(m, d):
+        size = 2**m
+        return leaf - place[m] + (place[m] + d) % size
+
+    def swap(name, m, d, src, dst):
+        k = SWAPS.index(name)
+        return pltpu.make_async_remote_copy(
+            src_ref=src, dst_ref=dst, send_sem=swap_send.at[k, d], recv_sem=swap_recv.at[k, d],
+            device_id=(peer(m, d), row), device_id_type=MESH)
+
+    def swap_start(name, m, src, dst, when=None):
+        size = 2**m
+        for d in range(1, size):
+            target = (place[m] + d) % size
+
+            def make(d=d, target=target):
+                return swap(name, m, d, src(target), dst(place[m], d))
+
+            if when is None:
+                make().start()
+                pending.append((None, make))
+            else:
+                can = when(target)
+
+                @pl.when(can)
+                def _(make=make):
+                    make().start()
+
+                pending.append((can, make))
+
+    def swap_wait(name, m, src, dst):
+        size = 2**m
+        for d in range(1, size):
+            sender = (place[m] - d + size) % size
+            swap(name, m, d, src(place[m]), dst(sender, d)).wait_recv()
+
+    def z0_slot(c):
+        return lambda q: z0.at[c, q]
+
+    def y0_slot(c):
+        return lambda q: y0.at[c, q]
+
+    def z1_slot(c):
+        return lambda q: z1.at[c, :, q]
+
+    def y1_slot(c):
+        return lambda q: y1.at[c, q]
+
+    def z2_slot(q):
+        return z2.at[:, q]
+
+    def y2_slot(q):
+        return y2.at[q]
+
+    def z3_slot(q):
+        return z3.at[:, q]
+
+    for c in range(CHUNKS):
+        gather_start("z0" + suffix[c], z0_slot(c), rhs.at[pl.ds(0, height), pl.ds(c * chunk, chunk)])
+
+    fixed = []
+    for c in range(CHUNKS):
+        fixed.append((
+            "b1" + suffix[c], 1,
+            lambda target, c=c: rhs.at[level_rows(1), at_cols(2 * c + target)],
+            lambda sender, d, c=c: b1.at[c, sender]))
+    fixed.append(("d1", 1, lambda target: inv.at[level_rows(1)], lambda sender, d: d1.at[sender]))
+    fixed.append(("b2", 2, lambda target: rhs.at[level_rows(2), at_cols(target)], lambda sender, d: b2.at[sender]))
+    fixed.append(("d2", 2, lambda target: inv.at[level_rows(2)], lambda sender, d: d2.at[sender]))
+    fixed.append(("b3", 3, lambda target: rhs.at[level_rows(3), at_cols(target // 2)], lambda sender, d: b3.at[sender]))
+    fixed.append(("d3", 3, lambda target: inv.at[level_rows(3)], lambda sender, d: d3.at[sender]))
+    for entry in fixed:
+        swap_start(*entry)
+
+    def live(pair):
+        return mask[pair].astype(jnp.float32)
+
+    def cols_of(c):
+        return pl.ds(c * chunk, chunk)
+
+    for step in range(1, rows_n - 1):
+        for c in range(CHUNKS):
+            gather_step("z0" + suffix[c], z0_slot(c), step)
+    local_copies["d0"].wait()
+    whole = d0.shape[1]
+    for c in range(CHUNKS):
+        local_copies["z0" + suffix[c]].wait()
+        gather_step("z0" + suffix[c], z0_slot(c), rows_n - 1)
+        solved = dot32(d0[...], z0[c].reshape(whole, chunk))
+        y0[c, row] = solved.astype(jnp.bfloat16)
+        gather_start("y0" + suffix[c], y0_slot(c))
+        out[pl.ds(0, height), cols_of(c)] = solved
+    for step in range(1, rows_n - 1):
+        for c in range(CHUNKS):
+            gather_step("y0" + suffix[c], y0_slot(c), step)
+    for name in ("p1", "p2", "p3"):
+        local_copies[name].wait()
+
+    for c in range(CHUNKS):
+        gather_step("y0" + suffix[c], y0_slot(c), rows_n - 1)
+        known = y0[c].reshape(whole, chunk)
+        update = dot32(p1[...], known) * live(0)
+        u1[c] = update
+        u1s[c] = update.astype(jnp.bfloat16)
+        name = "u1" + suffix[c]
+        src = lambda target, c=c: u1s.at[c, :, at_cols(target)]
+        dst = lambda sender, d, c=c: u1r.at[c, d - 1]
+        swap_start(name, 1, src, dst)
+        u2[:, cols_of(c)] = dot32(p2[:, :whole], known) * live(1)
+        local_copies["b1" + suffix[c]].wait()
+        swap_wait(*fixed[c])
+        swap_wait(name, 1, src, dst)
+        total = u1[c, :, at_cols(place[1])] + u1r[c, 0].astype(jnp.float32)
+        reduced = (b1[c].reshape(height, wide).astype(jnp.float32) - total).astype(jnp.bfloat16)
+        for s in range(2):
+            z1[c, s, row] = reduced[s * heights[1] : (s + 1) * heights[1]]
+        gather_start("z1" + suffix[c], z1_slot(c))
+        u3[:, cols_of(c)] = dot32(p3[:, :whole], known) * live(3)
+    for step in range(1, rows_n - 1):
+        for c in range(CHUNKS):
+            gather_step("z1" + suffix[c], z1_slot(c), step)
+    local_copies["d1"].wait()
+    swap_wait(*fixed[CHUNKS])
+    y1_src = [lambda target, c=c: y1s.at[c, target] for c in range(CHUNKS)]
+    y1_dst = [lambda sender, d, c=c: y1.at[c, row, :, at_cols(sender)] for c in range(CHUNKS)]
+    for c in range(CHUNKS):
+        gather_step("z1" + suffix[c], z1_slot(c), rows_n - 1)
+        solved = dot32(d1[...].reshape(height, whole), z1[c].reshape(whole, wide)).astype(jnp.bfloat16)
+        y1s[c] = solved.reshape(2, heights[1], wide)
+        swap_start("y1" + suffix[c], 1, y1_src[c], y1_dst[c])
+        y1[c, row, :, at_cols(place[1])] = y1s[c, place[1]]
+        swap_wait("y1" + suffix[c], 1, y1_src[c], y1_dst[c])
+        gather_start("y1" + suffix[c], y1_slot(c))
+        out[level_rows(1), cols_of(c)] = y1[c, row].astype(jnp.float32)
+    for step in range(1, rows_n - 1):
+        for c in range(CHUNKS):
+            gather_step("y1" + suffix[c], y1_slot(c), step)
+
+    half = whole // 2
+    u2_src = lambda target: u2s.at[:, at_cols(target)]
+    u2_dst = lambda sender, d: u2r.at[d - 1]
+    for c in range(CHUNKS):
+        gather_step("y1" + suffix[c], y1_slot(c), rows_n - 1)
+        known = y1[c].reshape(half, chunk)
+        update = u2[:, cols_of(c)] + dot32(p2[:, whole:], known) * live(2)
+        u2[:, cols_of(c)] = update
+        u2s[:, cols_of(c)] = update.astype(jnp.bfloat16)
+        swap_start("u2", 2, u2_src, u2_dst, lambda target, c=c: target // 2 == c)
+        u3[:, cols_of(c)] += dot32(p3[:, whole : whole + half], known) * live(4)
+    local_copies["b2"].wait()
+    swap_wait(*fixed[CHUNKS + 1])
+    swap_wait("u2", 2, u2_src, u2_dst)
+    total = u2[:, at_cols(place[2])]
+    for d in range(3):
+        total = total + u2r[d].astype(jnp.float32)
+    reduced = (b2[...].reshape(height, wide).astype(jnp.float32) - total).astype(jnp.bfloat16)
+    for s in range(4):
+        z2[s, row] = reduced[s * heights[2] : (s + 1) * heights[2]]
+    gather_start("z2", z2_slot)
+    local_copies["d2"].wait()
+    swap_wait(*fixed[CHUNKS + 2])
+    for step in range(1, rows_n):
+        gather_step("z2", z2_slot, step)
+    solved = dot32(d2[...].reshape(height, whole), z2[...].reshape(whole, wide)).astype(jnp.bfloat16)
+    y2s[...] = solved.reshape(4, heights[2], wide)
+    y2_src = lambda target: y2s.at[target]
+    y2_dst = lambda sender, d: y2.at[row, :, at_cols(sender)]
+    swap_start("y2", 2, y2_src, y2_dst)
+    y2[row, :, at_cols(place[2])] = y2s[place[2]]
+    swap_wait("y2", 2, y2_src, y2_dst)
+    gather_start("y2", y2_slot)
+    out[level_rows(2), :] = y2[row].astype(jnp.float32)
+    for step in range(1, rows_n):
+        gather_step("y2", y2_slot, step)
+
+    update = u3[...] + dot32(p3[:, whole + half :], y2[...].reshape(whole // 4, right_n)) * live(5)
+    fold = height // 2
+    low = lax.broadcasted_iota(jnp.int32, (fold, wide), 1) < wide // 2
+    def folded(top, bottom):
+        return (
+            jnp.where(low, top, pltpu.roll(bottom, wide // 2, 1)),
+            jnp.where(low, pltpu.roll(top, wide // 2, 1), bottom),
+        )
+    for k in range(leaves_n // 2):
+        pair = folded(update[:fold, k * wide : (k + 1) * wide], update[fold:, k * wide : (k + 1) * wide])
+        for side in range(2):
+            u3s[2 * k + side] = pair[side].astype(jnp.bfloat16)
+    u3_src = lambda target: u3s.at[target]
+    u3_dst = lambda sender, d: u3r.at[d - 1]
+    swap_start("u3", 3, u3_src, u3_dst)
+    local_copies["b3"].wait()
+    swap_wait(*fixed[CHUNKS + 3])
+    own_b = b3[...].astype(jnp.float32)
+    sides = folded(own_b[:4].reshape(fold, wide), own_b[4:].reshape(fold, wide))
+    own_b = jnp.where(place[3] % 2 == 0, sides[0], sides[1])
+    swap_wait("u3", 3, u3_src, u3_dst)
+    total = u3s[place[3]].astype(jnp.float32)
+    for d in range(leaves_n - 1):
+        total = total + u3r[d].astype(jnp.float32)
+    reduced = (own_b - total).astype(jnp.bfloat16)
+    for s in range(4):
+        z3[s, row] = reduced[s * heights[3] : (s + 1) * heights[3]]
+    gather_start("z3", z3_slot)
+    local_copies["d3"].wait()
+    swap_wait(*fixed[CHUNKS + 4])
+    for step in range(1, rows_n):
+        gather_step("z3", z3_slot, step)
+    known = z3[...].reshape(half, wide)
+    left = dot32(d3[:, :, :half].reshape(height, half), known)
+    right = dot32(d3[:, :, half:].reshape(height, half), known)
+    solved = left + pltpu.roll(right, wide // 2, 1)
+    low_all = lax.broadcasted_iota(jnp.int32, (height, wide), 1) < wide // 2
+    solved = jnp.where(low_all, solved, pltpu.roll(solved, wide // 2, 1))
+    y3s[...] = solved.astype(jnp.bfloat16).reshape(leaves_n, heights[3], wide)
+    y3_src = lambda target: y3s.at[target]
+    y3_dst = lambda sender, d: y3r.at[sender]
+    swap_start("y3", 3, y3_src, y3_dst)
+    y3r[place[3]] = y3s[place[3]]
+    swap_wait("y3", 3, y3_src, y3_dst)
+    low_out = lax.broadcasted_iota(jnp.int32, (heights[3], wide), 1) < wide // 2
+    for k in range(leaves_n // 2):
+        out[level_rows(3), pl.ds(k * wide, wide)] = jnp.where(
+            low_out, y3r[2 * k].astype(jnp.float32), y3r[2 * k + 1].astype(jnp.float32))
+
+    for can, make in pending:
+        if can is None:
+            make().wait_send()
+        else:
+            @pl.when(can)
+            def _(make=make):
+                make().wait_send()
+
+
+def fits(rows_n, leaves_n, rhs, inv_diag, off_diag):
+    whole = inv_diag.shape[3]
+    right_n = rhs.shape[3]
+    return (
+        leaves_n == 2**TREE_LEVELS
+        and rows_n > 1
+        and whole % (leaves_n * rows_n * ROW_TILE) == 0
+        and whole % (4 * LANES) == 0
+        and right_n == 4 * LANES
+    )
+
+
+def tree_shards(rhs, inv_diag, off_diag, pair_mask):
+    rows_n = lax.axis_size("row")
+    leaves_n = lax.axis_size("leaf")
+    whole = inv_diag.shape[3]
+    right_n = rhs.shape[3]
+    height = off_diag.shape[2]
+    chunk = right_n // CHUNKS
+    hs = [height // 2**m for m in range(TREE_LEVELS + 1)]
+    bf16, f32 = jnp.bfloat16, jnp.float32
+    vm = pltpu.VMEM
+    scratch = [
+        vm((height, whole), bf16),
+        vm((2, hs[1], whole), bf16), vm((4, hs[2], whole), bf16), vm((8, hs[3], whole), bf16),
+        vm((height, whole), bf16), vm((height, whole + whole // 2), bf16),
+        vm((height, whole + whole // 2 + whole // 4), bf16),
+        vm((CHUNKS, 2, hs[1], LANES), bf16), vm((4, hs[2], LANES), bf16), vm((8, hs[3], LANES), bf16),
+        vm((CHUNKS, rows_n, height, chunk), bf16),
+        vm((CHUNKS, 2, rows_n, hs[1], LANES), bf16),
+        vm((4, rows_n, hs[2], LANES), bf16),
+        vm((4, rows_n, hs[3], LANES), bf16),
+        vm((CHUNKS, rows_n, height, chunk), bf16),
+        vm((CHUNKS, rows_n, hs[1], chunk), bf16),
+        vm((rows_n, hs[2], right_n), bf16),
+        vm((CHUNKS, height, chunk), f32), vm((height, right_n), f32), vm((height, right_n), f32),
+        vm((CHUNKS, height, chunk), bf16), vm((height, right_n), bf16),
+        vm((leaves_n, height // 2, LANES), bf16),
+        vm((CHUNKS, 1, height, LANES), bf16), vm((3, height, LANES), bf16),
+        vm((leaves_n - 1, height // 2, LANES), bf16),
+        vm((CHUNKS, 2, hs[1], LANES), bf16), vm((4, hs[2], LANES), bf16),
+        vm((leaves_n, hs[3], LANES), bf16), vm((leaves_n, hs[3], LANES), bf16),
+        pltpu.SemaphoreType.DMA((len(GATHERS), rows_n)),
+        pltpu.SemaphoreType.DMA((len(GATHERS), rows_n)),
+        pltpu.SemaphoreType.DMA((len(GATHERS), rows_n)),
+        pltpu.SemaphoreType.DMA((len(SWAPS), leaves_n)),
+        pltpu.SemaphoreType.DMA((len(SWAPS), leaves_n)),
+        pltpu.SemaphoreType.DMA((len(LOCALS),)),
+    ]
+    pack = rhs.shape[2]
+    flops = 2 * right_n * (pack * whole + height * off_diag.shape[3])
+    moved = 2 * (pack * whole + height * off_diag.shape[3] + 3 * pack * right_n)
+    solved = pl.pallas_call(
+        functools.partial(tree_kernel, rows_n, leaves_n),
+        out_shape=jax.ShapeDtypeStruct((pack, right_n), f32),
+        in_specs=[pl.BlockSpec(memory_space=pltpu.SMEM)] + [pl.BlockSpec(memory_space=pl.ANY)] * 3,
+        out_specs=pl.BlockSpec(memory_space=pltpu.VMEM),
+        scratch_shapes=scratch,
+        compiler_params=pltpu.CompilerParams(
+            collective_id=0, has_side_effects=True, vmem_limit_bytes=48 * 2**20),
+        cost_estimate=pl.CostEstimate(flops=flops, bytes_accessed=moved, transcendentals=0),
+    )(pair_mask[0, 0], rhs[0, 0], inv_diag[0, 0], off_diag[0, 0])
+    return solved[None, None]
+
+
 def solution(mesh):
     in_specs = (
         P("leaf", "row", None, None),
@@ -93,4 +514,12 @@
         P("leaf", "row", None),
     )
     out_specs = P("leaf", "row", None, None)
-    return jax.shard_map(shards, mesh=mesh, in_specs=in_specs, out_specs=out_specs, check_vma=False)
+
+    def run(rhs, inv_diag, off_diag, pair_mask):
+        fit = fits(mesh.shape["row"], mesh.shape["leaf"], rhs, inv_diag, off_diag)
+        body = tree_shards if fit else shards
+        return jax.shard_map(body, mesh=mesh, in_specs=in_specs, out_specs=out_specs, check_vma=False)(
+            rhs, inv_diag, off_diag, pair_mask
+        )
+
+    return run

time: 273 us -> 145 us (0.53)
  Pallas kernels: 0 us -> 140 us
  waiting for transfers between devices: 139 us -> 0 us
  blocking collectives: 78.9 us -> 0 us
  matrix products: 18.3 us -> 0 us
  between operations: 13.7 us -> 0.01 us
  starting transfers between devices: 11.3 us -> 0 us
  other arithmetic: 8.65 us -> 0 us
    pallas_call x0 -> x1, Pallas kernels: none -> 140 us  [tree_shards(): pl.pallas_call(functools.partial(tree_kernel, rows_n, leaves_n), out_shap...]
    all_gather x5 -> x0, blocking collectives: 78.9 us -> none  [the longest x3 46.5 us: shards(): gathered = lax.all_gather(reduced, 'row', axis=0, tiled=True)]
    all_gather x2 -> x0, waiting for transfers between devices: 75.8 us -> none  [the longest x1 40.4 us: shards(): gathered = lax.all_gather(reduced, 'row', axis=0, tiled=True)]
    ppermute x12 -> x0, waiting for transfers between devices: 63.3 us -> none  [partner_2(): return lax.ppermute(block, axis, route)]
    dot_general x7 -> x0, matrix products: 18.3 us -> none  [the longest x4 9.82 us: shards(): solved = jnp.dot(own_inv, gathered, preferred_element_type=jnp.float32)]
    ppermute x12 -> x0, starting transfers between devices: 11.3 us -> none  [partner_2(): return lax.ppermute(block, axis, route)]
    unnamed x6 -> x7, local copies, waits for them, and re-layouts: 0.02 us -> 4.51 us
    mul x3 -> x0, other arithmetic: 3.47 us -> none  [shards(): known_parts[source] * live_pairs[ancestor * (ancestor - 1) // 2 + source]]
  transfers between devices with their start and end apart: 14 -> 0, of which waited for: 14 -> 0; matrix products, arithmetic and copies ran while one was open for 1% -> 0% of each run, Pallas kernels for 0% -> 0%
where the time goes in v1:
time: 145 us
  Pallas kernels  140 us (97%)
  local copies, waits for them, and re-layouts  4.51 us (3%)
    pallas_call x1, Pallas kernels, tree_shards(): pl.pallas_call(functools.partial(tree_kernel, rows_n, leaves_n), out_shap...  140 us
    unnamed x7, local copies, waits for them, and re-layouts  4.51 us

profile of v1, /device:TPU:0, one launch (start us, length us, event | category | flops | bytes accessed | tf_op | source)
XLA Modules:
  0.0 144.7 jit_solution(621320553839552739)
XLA Ops:
  0.0 0.0 copy-start
  0.0 1.6 %copy-done = bf16[1,1,720,1536]{3,2,1,0:T(8,128)(2,1)S(1)} copy-done((bf16[1,1,720,1536]{3,2,1,0:T(8,128)(2,1)S(1)}, bf16[1,1,720,1536]{3,2,1,0:T(8,128)(2,1)}, u32[]{:S(2)}) %copy-start) | copy-done | bytes 2211864
  1.6 0.0 copy-start.1
  1.6 1.1 copy-done.1
  2.7 0.0 copy-start.2
  2.7 0.7 copy-done.2
  3.4 140.2 %shard_map.46 = f32[720,512]{1,0:T(8,128)S(1)} custom-call(s32[6]{0:T(128)S(1)} %bitcast.8, bf16[720,512]{1,0:T(8,128)(2,1)S(1)} %bitcast.7, bf16[720,1536]{1,0:T(8,128)(2,1)S(1)} %bitcast.6, bf16[384,6528]{1,0:T(8,128)(2,1)} %bitcast.9), custom_call_target="tpu_custom_call" | custom-call | flops 3699376128 | bytes 9437184 | tf_op jit(solution)/shard_map/pallas_call | solution.py:496
  143.6 1.1 copy.6
Async XLA Ops:
  0.0 1.6 %copy-start = (bf16[1,1,720,1536]{3,2,1,0:T(8,128)(2,1)S(1)}, bf16[1,1,720,1536]{3,2,1,0:T(8,128)(2,1)}, u32[]{:S(2)}) copy-start(bf16[1,1,720,1536]{3,2,1,0:T(8,128)(2,1)} %param.5) | copy-start | bytes 6635524
  1.6 1.1 copy-start.1
  2.7 0.7 copy-start.2

commit v2 on v1

--- a/solution.py
+++ b/solution.py
@@ -99,8 +99,8 @@
     return jnp.dot(left, right, preferred_element_type=jnp.float32)
 
 
-GATHERS = ["z0a", "z0b", "y0a", "y0b", "z1a", "z1b", "y1a", "y1b", "z2", "y2", "z3"]
-SWAPS = ["b1a", "b1b", "b2", "b3", "d1", "d2", "d3", "u1a", "u1b", "u2", "u3", "y1a", "y1b", "y2", "y3"]
+GATHERS = ["z0a", "z0b", "y0a", "y0b", "z1a", "z1b", "y1a", "y1b", "z2", "z3"]
+SWAPS = ["b1a", "b1b", "b2", "b3", "d1", "d2", "d3", "u1a", "u1b", "u2", "u3", "y1a", "y1b", "y3"]
 LOCALS = ["z0a", "z0b", "d0", "p1", "p2", "p3", "d1", "d2", "d3", "b1a", "b1b", "b2", "b3"]
 
 
@@ -110,7 +110,7 @@
     d0, d1, d2, d3, p1, p2, p3, b1, b2, b3,
     z0, z1, z2, z3, y0, y1, y2,
     u1, u2, u3, u1s, u2s, u3s, u1r, u2r, u3r, y1s, y2s, y3s, y3r,
-    up_sem, down_sem, land_sem, swap_send, swap_recv, local_sem,
+    up_sem, down_sem, land_sem, swap_send, swap_recv, local_sem, spread_send, spread_recv,
 ):
     leaf = lax.axis_index("leaf")
     row = lax.axis_index("row")
@@ -123,6 +123,10 @@
     suffix = "ab"
     pending = []
     place = [leaf % 2**m for m in range(TREE_LEVELS + 1)]
+    own_chunk = leaf % 2
+
+    def block_of(position):
+        return 2 * (position % 2) + position // 2 % 2
 
     def at_cols(index):
         return pl.ds(pl.multiple_of(index * wide, wide), wide)
@@ -132,14 +136,11 @@
 
     barrier = pltpu.get_barrier_semaphore()
 
-    @pl.when(row < rows_n - 1)
-    def _():
-        pl.semaphore_signal(barrier, inc=1, device_id=(leaf, row + 1), device_id_type=MESH)
-
-    @pl.when(row > 0)
-    def _():
-        pl.semaphore_signal(barrier, inc=1, device_id=(leaf, row - 1), device_id_type=MESH)
-
+    for e in range(1, rows_n):
+        for d in range(4):
+            pl.semaphore_signal(
+                barrier, inc=1, device_id=(leaf - place[2] + (place[2] + d) % 4, (row + e) % rows_n),
+                device_id_type=MESH)
     for d in range(1, leaves_n):
         pl.semaphore_signal(barrier, inc=1, device_id=((leaf + d) % leaves_n, row), device_id_type=MESH)
 
@@ -159,15 +160,21 @@
     for c in range(CHUNKS):
         local_copies["b1" + suffix[c]] = local(
             "b1" + suffix[c], rhs.at[level_rows(1), at_cols(2 * c + place[1])], b1.at[c, place[1]])
-    local_copies["b2"] = local("b2", rhs.at[level_rows(2), at_cols(place[2])], b2.at[place[2]])
-    local_copies["b3"] = local("b3", rhs.at[level_rows(3), at_cols(place[3] // 2)], b3.at[place[3]])
+    local_copies["b2"] = local("b2", rhs.at[level_rows(2), at_cols(block_of(place[2]))], b2.at[place[2]])
+    local_copies["b3"] = local("b3", rhs.at[level_rows(3), at_cols(block_of(place[3]))], b3.at[place[3]])
     for name in LOCALS:
         local_copies[name].start()
 
-    def hops():
-        return jnp.where(row > 0, 1, 0) + jnp.where(row < rows_n - 1, 1, 0)
-
-    pl.semaphore_wait(barrier, hops() + leaves_n - 1)
+    pl.semaphore_wait(barrier, 4 * (rows_n - 1) + leaves_n - 1)
+
+    def begin(can, make):
+        if can is None:
+            make().start()
+        else:
+            @pl.when(can)
+            def _():
+                make().start()
+        pending.append((can, make))
 
     def hop(name, src, dst, step, source, way):
         k = GATHERS.index(name)
@@ -208,6 +215,24 @@
 
                 pending.append((both, make))
 
+    def direct(name, slot, e):
+        k = GATHERS.index(name)
+        return pltpu.make_async_remote_copy(
+            src_ref=slot(row), dst_ref=slot(row), send_sem=up_sem.at[k, e], recv_sem=land_sem.at[k, e],
+            device_id=(leaf, (row + e) % rows_n), device_id_type=MESH)
+
+    def direct_start(name, slot, can):
+        for e in range(1, rows_n):
+            begin(can, lambda e=e: direct(name, slot, e))
+
+    def direct_wait(name, slot):
+        k = GATHERS.index(name)
+        for e in range(1, rows_n):
+            there = slot((row - e + rows_n) % rows_n)
+            pltpu.make_async_remote_copy(
+                src_ref=there, dst_ref=there, send_sem=up_sem.at[k, e], recv_sem=land_sem.at[k, e],
+                device_id=(leaf, (row + e) % rows_n), device_id_type=MESH).wait_recv()
+
     def peer(m, d):
         size = 2**m
         return leaf - place[m] + (place[m] + d) % size
@@ -226,17 +251,7 @@
             def make(d=d, target=target):
                 return swap(name, m, d, src(target), dst(place[m], d))
 
-            if when is None:
-                make().start()
-                pending.append((None, make))
-            else:
-                can = when(target)
-
-                @pl.when(can)
-                def _(make=make):
-                    make().start()
-
-                pending.append((can, make))
+            begin(None if when is None else when(target), make)
 
     def swap_wait(name, m, src, dst):
         size = 2**m
@@ -258,9 +273,6 @@
 
     def z2_slot(q):
         return z2.at[:, q]
-
-    def y2_slot(q):
-        return y2.at[q]
 
     def z3_slot(q):
         return z3.at[:, q]
@@ -275,9 +287,9 @@
             lambda target, c=c: rhs.at[level_rows(1), at_cols(2 * c + target)],
             lambda sender, d, c=c: b1.at[c, sender]))
     fixed.append(("d1", 1, lambda target: inv.at[level_rows(1)], lambda sender, d: d1.at[sender]))
-    fixed.append(("b2", 2, lambda target: rhs.at[level_rows(2), at_cols(target)], lambda sender, d: b2.at[sender]))
+    fixed.append(("b2", 2, lambda target: rhs.at[level_rows(2), at_cols(block_of(target))], lambda sender, d: b2.at[sender]))
     fixed.append(("d2", 2, lambda target: inv.at[level_rows(2)], lambda sender, d: d2.at[sender]))
-    fixed.append(("b3", 3, lambda target: rhs.at[level_rows(3), at_cols(target // 2)], lambda sender, d: b3.at[sender]))
+    fixed.append(("b3", 3, lambda target: rhs.at[level_rows(3), at_cols(block_of(target))], lambda sender, d: b3.at[sender]))
     fixed.append(("d3", 3, lambda target: inv.at[level_rows(3)], lambda sender, d: d3.at[sender]))
     for entry in fixed:
         swap_start(*entry)
@@ -306,131 +318,211 @@
     for name in ("p1", "p2", "p3"):
         local_copies[name].wait()
 
-    for c in range(CHUNKS):
+    half = whole // 2
+    u1_src = [lambda target, c=c: u1s.at[c, :, at_cols(target)] for c in range(CHUNKS)]
+    u1_dst = [lambda sender, d, c=c: u1r.at[c, d - 1] for c in range(CHUNKS)]
+    y1_src = [lambda target, c=c: y1s.at[c, target] for c in range(CHUNKS)]
+    y1_dst = [lambda sender, d, c=c: y1.at[c, row, :, at_cols(sender)] for c in range(CHUNKS)]
+
+    def update_1(c):
         gather_step("y0" + suffix[c], y0_slot(c), rows_n - 1)
-        known = y0[c].reshape(whole, chunk)
-        update = dot32(p1[...], known) * live(0)
+        update = dot32(p1[...], y0[c].reshape(whole, chunk)) * live(0)
         u1[c] = update
         u1s[c] = update.astype(jnp.bfloat16)
-        name = "u1" + suffix[c]
-        src = lambda target, c=c: u1s.at[c, :, at_cols(target)]
-        dst = lambda sender, d, c=c: u1r.at[c, d - 1]
-        swap_start(name, 1, src, dst)
-        u2[:, cols_of(c)] = dot32(p2[:, :whole], known) * live(1)
+        swap_start("u1" + suffix[c], 1, u1_src[c], u1_dst[c])
+
+    def reduce_1(c):
         local_copies["b1" + suffix[c]].wait()
         swap_wait(*fixed[c])
-        swap_wait(name, 1, src, dst)
+        swap_wait("u1" + suffix[c], 1, u1_src[c], u1_dst[c])
         total = u1[c, :, at_cols(place[1])] + u1r[c, 0].astype(jnp.float32)
         reduced = (b1[c].reshape(height, wide).astype(jnp.float32) - total).astype(jnp.bfloat16)
         for s in range(2):
             z1[c, s, row] = reduced[s * heights[1] : (s + 1) * heights[1]]
         gather_start("z1" + suffix[c], z1_slot(c))
-        u3[:, cols_of(c)] = dot32(p3[:, :whole], known) * live(3)
-    for step in range(1, rows_n - 1):
-        for c in range(CHUNKS):
-            gather_step("z1" + suffix[c], z1_slot(c), step)
-    local_copies["d1"].wait()
-    swap_wait(*fixed[CHUNKS])
-    y1_src = [lambda target, c=c: y1s.at[c, target] for c in range(CHUNKS)]
-    y1_dst = [lambda sender, d, c=c: y1.at[c, row, :, at_cols(sender)] for c in range(CHUNKS)]
-    for c in range(CHUNKS):
+
+    def early_2(c):
+        u2[:, cols_of(c)] = dot32(p2[:, :whole], y0[c].reshape(whole, chunk)) * live(1)
+
+    def early_3(c):
+        u3[:, cols_of(c)] = dot32(p3[:, :whole], y0[c].reshape(whole, chunk)) * live(3)
+
+    def solve_1(c):
         gather_step("z1" + suffix[c], z1_slot(c), rows_n - 1)
         solved = dot32(d1[...].reshape(height, whole), z1[c].reshape(whole, wide)).astype(jnp.bfloat16)
         y1s[c] = solved.reshape(2, heights[1], wide)
         swap_start("y1" + suffix[c], 1, y1_src[c], y1_dst[c])
         y1[c, row, :, at_cols(place[1])] = y1s[c, place[1]]
+
+    def spread_1(c):
         swap_wait("y1" + suffix[c], 1, y1_src[c], y1_dst[c])
         gather_start("y1" + suffix[c], y1_slot(c))
-        out[level_rows(1), cols_of(c)] = y1[c, row].astype(jnp.float32)
-    for step in range(1, rows_n - 1):
-        for c in range(CHUNKS):
-            gather_step("y1" + suffix[c], y1_slot(c), step)
-
-    half = whole // 2
-    u2_src = lambda target: u2s.at[:, at_cols(target)]
+
+    u2_src = lambda target: u2s.at[:, at_cols(block_of(target))]
     u2_dst = lambda sender, d: u2r.at[d - 1]
-    for c in range(CHUNKS):
+
+    def update_2(c):
         gather_step("y1" + suffix[c], y1_slot(c), rows_n - 1)
-        known = y1[c].reshape(half, chunk)
-        update = u2[:, cols_of(c)] + dot32(p2[:, whole:], known) * live(2)
+        update = u2[:, cols_of(c)] + dot32(p2[:, whole:], y1[c].reshape(half, chunk)) * live(2)
         u2[:, cols_of(c)] = update
         u2s[:, cols_of(c)] = update.astype(jnp.bfloat16)
-        swap_start("u2", 2, u2_src, u2_dst, lambda target, c=c: target // 2 == c)
-        u3[:, cols_of(c)] += dot32(p3[:, whole : whole + half], known) * live(4)
-    local_copies["b2"].wait()
-    swap_wait(*fixed[CHUNKS + 1])
-    swap_wait("u2", 2, u2_src, u2_dst)
-    total = u2[:, at_cols(place[2])]
-    for d in range(3):
-        total = total + u2r[d].astype(jnp.float32)
-    reduced = (b2[...].reshape(height, wide).astype(jnp.float32) - total).astype(jnp.bfloat16)
-    for s in range(4):
-        z2[s, row] = reduced[s * heights[2] : (s + 1) * heights[2]]
-    gather_start("z2", z2_slot)
-    local_copies["d2"].wait()
-    swap_wait(*fixed[CHUNKS + 2])
-    for step in range(1, rows_n):
-        gather_step("z2", z2_slot, step)
-    solved = dot32(d2[...].reshape(height, whole), z2[...].reshape(whole, wide)).astype(jnp.bfloat16)
-    y2s[...] = solved.reshape(4, heights[2], wide)
-    y2_src = lambda target: y2s.at[target]
-    y2_dst = lambda sender, d: y2.at[row, :, at_cols(sender)]
-    swap_start("y2", 2, y2_src, y2_dst)
-    y2[row, :, at_cols(place[2])] = y2s[place[2]]
-    swap_wait("y2", 2, y2_src, y2_dst)
-    gather_start("y2", y2_slot)
-    out[level_rows(2), :] = y2[row].astype(jnp.float32)
-    for step in range(1, rows_n):
-        gather_step("y2", y2_slot, step)
-
-    update = u3[...] + dot32(p3[:, whole + half :], y2[...].reshape(whole // 4, right_n)) * live(5)
+        swap_start("u2", 2, u2_src, u2_dst, lambda target: target % 2 == c)
+
+    def later_3(c):
+        u3[:, cols_of(c)] += dot32(p3[:, whole : whole + half], y1[c].reshape(half, chunk)) * live(4)
+
+    def reduce_2(c):
+        @pl.when(own_chunk == c)
+        def _():
+            swap_wait("u2", 2, u2_src, u2_dst)
+            total = u2[:, at_cols(block_of(place[2]))]
+            for d in range(3):
+                total = total + u2r[d].astype(jnp.float32)
+            reduced = (b2[...].reshape(height, wide).astype(jnp.float32) - total).astype(jnp.bfloat16)
+            for s in range(4):
+                z2[s, row] = reduced[s * heights[2] : (s + 1) * heights[2]]
+
+        direct_start("z2", z2_slot, own_chunk == c)
+
+    def spread(d, e, position):
+        here = leaf - place[2] + (place[2] + d) % 4
+        dst = y2.at[(row if position is None else (row - e + rows_n) % rows_n), :,
+                    at_cols(block_of(place[2] if position is None else position))]
+        src = y2s.at[(place[2] + d) % 4]
+        return pltpu.make_async_remote_copy(
+            src_ref=src, dst_ref=dst, send_sem=spread_send.at[d, e], recv_sem=spread_recv.at[d, e],
+            device_id=(here, (row + e) % rows_n), device_id_type=MESH)
+
+    others = [(d, e) for e in reversed(range(rows_n)) for d in range(4) if d or e]
+
+    def solve_2(c):
+        @pl.when(own_chunk == c)
+        def _():
+            direct_wait("z2", z2_slot)
+            solved = dot32(d2[...].reshape(height, whole), z2[...].reshape(whole, wide)).astype(jnp.bfloat16)
+            y2s[...] = solved.reshape(4, heights[2], wide)
+
+        for d, e in others:
+            begin(own_chunk == c, lambda d=d, e=e: spread(d, e, None))
+
+        @pl.when(own_chunk == c)
+        def _():
+            y2[row, :, at_cols(block_of(place[2]))] = y2s[place[2]]
+
     fold = height // 2
     low = lax.broadcasted_iota(jnp.int32, (fold, wide), 1) < wide // 2
+
     def folded(top, bottom):
         return (
             jnp.where(low, top, pltpu.roll(bottom, wide // 2, 1)),
             jnp.where(low, pltpu.roll(top, wide // 2, 1), bottom),
         )
-    for k in range(leaves_n // 2):
-        pair = folded(update[:fold, k * wide : (k + 1) * wide], update[fold:, k * wide : (k + 1) * wide])
-        for side in range(2):
-            u3s[2 * k + side] = pair[side].astype(jnp.bfloat16)
+
     u3_src = lambda target: u3s.at[target]
     u3_dst = lambda sender, d: u3r.at[d - 1]
-    swap_start("u3", 3, u3_src, u3_dst)
+
+    def update_3(c):
+        for d, e in others:
+            sender = (place[2] - d + 4) % 4
+
+            @pl.when(sender % 2 == c)
+            def _(d=d, e=e, sender=sender):
+                spread(d, e, sender).wait_recv()
+
+        known = y2[:, :, c * chunk : (c + 1) * chunk].reshape(whole // 4, chunk)
+        update = u3[:, cols_of(c)] + dot32(p3[:, whole + half :], known) * live(5)
+        for k in range(2):
+            block = update[:, k * wide : (k + 1) * wide]
+            sides = folded(block[:fold], block[fold:])
+            for side in range(2):
+                u3s[4 * side + 2 * k + c] = sides[side].astype(jnp.bfloat16)
+        swap_start("u3", 3, u3_src, u3_dst, lambda target: target % 2 == c)
+
+    def reduce_3(c):
+        @pl.when(own_chunk == c)
+        def _():
+            own_b = b3[...].astype(jnp.float32)
+            sides = folded(own_b[:4].reshape(fold, wide), own_b[4:].reshape(fold, wide))
+            own_b = jnp.where(place[3] < leaves_n // 2, sides[0], sides[1])
+            swap_wait("u3", 3, u3_src, u3_dst)
+            total = u3s[place[3]].astype(jnp.float32)
+            for d in range(leaves_n - 1):
+                total = total + u3r[d].astype(jnp.float32)
+            reduced = (own_b - total).astype(jnp.bfloat16)
+            for s in range(4):
+                z3[s, row] = reduced[s * heights[3] : (s + 1) * heights[3]]
+
+        direct_start("z3", z3_slot, own_chunk == c)
+
+    y3_src = lambda target: y3s.at[target]
+    y3_dst = lambda sender, d: y3r.at[sender]
+
+    def solve_3():
+        direct_wait("z3", z3_slot)
+        known = z3[...].reshape(half, wide)
+        left = dot32(d3[:, :, :half].reshape(height, half), known)
+        right = dot32(d3[:, :, half:].reshape(height, half), known)
+        solved = left + pltpu.roll(right, wide // 2, 1)
+        low_all = lax.broadcasted_iota(jnp.int32, (height, wide), 1) < wide // 2
+        solved = jnp.where(low_all, solved, pltpu.roll(solved, wide // 2, 1))
+        y3s[...] = solved.astype(jnp.bfloat16).reshape(leaves_n, heights[3], wide)
+        swap_start("y3", 3, y3_src, y3_dst)
+        y3r[place[3]] = y3s[place[3]]
+
+    update_1(0)
+    early_2(0)
+    reduce_1(0)
+    early_3(0)
+    update_1(1)
+    gather_step("z1a", z1_slot(0), 1)
+    reduce_1(1)
+    early_2(1)
+    early_3(1)
+    for step in range(2, rows_n - 1):
+        gather_step("z1a", z1_slot(0), step)
+        gather_step("z1b", z1_slot(1), step - 1)
+    local_copies["d1"].wait()
+    swap_wait(*fixed[CHUNKS])
+    solve_1(0)
+    gather_step("z1b", z1_slot(1), rows_n - 2)
+    spread_1(0)
+    solve_1(1)
+    gather_step("y1a", y1_slot(0), 1)
+    spread_1(1)
+    for step in range(2, rows_n - 1):
+        gather_step("y1a", y1_slot(0), step)
+        gather_step("y1b", y1_slot(1), step - 1)
+    local_copies["b2"].wait()
+    swap_wait(*fixed[CHUNKS + 1])
+    update_2(0)
+    gather_step("y1b", y1_slot(1), rows_n - 2)
+    later_3(0)
+    reduce_2(0)
+    update_2(1)
+    local_copies["d2"].wait()
+    swap_wait(*fixed[CHUNKS + 2])
+    reduce_2(1)
+    later_3(1)
+    for c in range(CHUNKS):
+        out[level_rows(1), cols_of(c)] = y1[c, row].astype(jnp.float32)
     local_copies["b3"].wait()
     swap_wait(*fixed[CHUNKS + 3])
-    own_b = b3[...].astype(jnp.float32)
-    sides = folded(own_b[:4].reshape(fold, wide), own_b[4:].reshape(fold, wide))
-    own_b = jnp.where(place[3] % 2 == 0, sides[0], sides[1])
-    swap_wait("u3", 3, u3_src, u3_dst)
-    total = u3s[place[3]].astype(jnp.float32)
-    for d in range(leaves_n - 1):
-        total = total + u3r[d].astype(jnp.float32)
-    reduced = (own_b - total).astype(jnp.bfloat16)
-    for s in range(4):
-        z3[s, row] = reduced[s * heights[3] : (s + 1) * heights[3]]
-    gather_start("z3", z3_slot)
     local_copies["d3"].wait()
     swap_wait(*fixed[CHUNKS + 4])
-    for step in range(1, rows_n):
-        gather_step("z3", z3_slot, step)
-    known = z3[...].reshape(half, wide)
-    left = dot32(d3[:, :, :half].reshape(height, half), known)
-    right = dot32(d3[:, :, half:].reshape(height, half), known)
-    solved = left + pltpu.roll(right, wide // 2, 1)
-    low_all = lax.broadcasted_iota(jnp.int32, (height, wide), 1) < wide // 2
-    solved = jnp.where(low_all, solved, pltpu.roll(solved, wide // 2, 1))
-    y3s[...] = solved.astype(jnp.bfloat16).reshape(leaves_n, heights[3], wide)
-    y3_src = lambda target: y3s.at[target]
-    y3_dst = lambda sender, d: y3r.at[sender]
-    swap_start("y3", 3, y3_src, y3_dst)
-    y3r[place[3]] = y3s[place[3]]
+    solve_2(0)
+    solve_2(1)
+    update_3(0)
+    reduce_3(0)
+    update_3(1)
+    reduce_3(1)
+    out[level_rows(2), :] = y2[row].astype(jnp.float32)
+    solve_3()
     swap_wait("y3", 3, y3_src, y3_dst)
     low_out = lax.broadcasted_iota(jnp.int32, (heights[3], wide), 1) < wide // 2
     for k in range(leaves_n // 2):
+        first = 2 * (k % 2) + k // 2
         out[level_rows(3), pl.ds(k * wide, wide)] = jnp.where(
-            low_out, y3r[2 * k].astype(jnp.float32), y3r[2 * k + 1].astype(jnp.float32))
+            low_out, y3r[first].astype(jnp.float32), y3r[first + leaves_n // 2].astype(jnp.float32))
 
     for can, make in pending:
         if can is None:
@@ -446,7 +538,7 @@
     right_n = rhs.shape[3]
     return (
         leaves_n == 2**TREE_LEVELS
-        and rows_n > 1
+        and rows_n > 2
         and whole % (leaves_n * rows_n * ROW_TILE) == 0
         and whole % (4 * LANES) == 0
         and right_n == 4 * LANES
@@ -489,6 +581,8 @@
         pltpu.SemaphoreType.DMA((len(SWAPS), leaves_n)),
         pltpu.SemaphoreType.DMA((len(SWAPS), leaves_n)),
         pltpu.SemaphoreType.DMA((len(LOCALS),)),
+        pltpu.SemaphoreType.DMA((4, rows_n)),
+        pltpu.SemaphoreType.DMA((4, rows_n)),
     ]
     pack = rhs.shape[2]
     flops = 2 * right_n * (pack * whole + height * off_diag.shape[3])
@@ -496,7 +590,7 @@
     solved = pl.pallas_call(
         functools.partial(tree_kernel, rows_n, leaves_n),
         out_shape=jax.ShapeDtypeStruct((pack, right_n), f32),
-        in_specs=[pl.BlockSpec(memory_space=pltpu.SMEM)] + [pl.BlockSpec(memory_space=pl.ANY)] * 3,
+        in_specs=[pl.BlockSpec(memory_space=pltpu.SMEM)] + [pl.BlockSpec(memory_space=pltpu.HBM)] * 3,
         out_specs=pl.BlockSpec(memory_space=pltpu.VMEM),
         scratch_shapes=scratch,
         compiler_params=pltpu.CompilerParams(

time: 145 us -> 132 us (0.910)
  Pallas kernels: 140 us -> 127 us
    pallas_call x1, Pallas kernels: 140 us -> 127 us  [tree_shards(): pl.pallas_call(functools.partial(tree_kernel, rows_n, leaves_n), out_shap...]
where the time goes in v2:
time: 132 us
  Pallas kernels  127 us (96%)
  local copies, waits for them, and re-layouts  4.51 us (3%)
    pallas_call x1, Pallas kernels, tree_shards(): pl.pallas_call(functools.partial(tree_kernel, rows_n, leaves_n), out_shap...  127 us
    unnamed x7, local copies, waits for them, and re-layouts  4.51 us

profile of v2, /device:TPU:0, one launch (start us, length us, event | category | flops | bytes accessed | tf_op | source)
XLA Modules:
  0.0 131.8 jit_solution(17924115445493189064)
XLA Ops:
  0.0 0.0 copy-start
  0.0 1.6 %copy-done = bf16[1,1,720,1536]{3,2,1,0:T(8,128)(2,1)S(1)} copy-done((bf16[1,1,720,1536]{3,2,1,0:T(8,128)(2,1)S(1)}, bf16[1,1,720,1536]{3,2,1,0:T(8,128)(2,1)}, u32[]{:S(2)}) %copy-start) | copy-done | bytes 2211864
  1.6 0.0 copy-start.1
  1.6 1.1 copy-done.1
  2.7 0.0 copy-start.2
  2.7 0.7 copy-done.2
  3.4 127.3 %shard_map.46 = f32[720,512]{1,0:T(8,128)S(1)} custom-call(s32[6]{0:T(128)S(1)} %bitcast.8, bf16[720,512]{1,0:T(8,128)(2,1)S(1)} %bitcast.7, bf16[720,1536]{1,0:T(8,128)(2,1)S(1)} %bitcast.6, bf16[384,6528]{1,0:T(8,128)(2,1)} %bitcast.9), custom_call_target="tpu_custom_call" | custom-call | flops 3699376128 | bytes 9437184 | tf_op jit(solution)/shard_map/pallas_call | solution.py:590
  130.7 1.1 copy.6
Async XLA Ops:
  0.0 1.6 %copy-start = (bf16[1,1,720,1536]{3,2,1,0:T(8,128)(2,1)S(1)}, bf16[1,1,720,1536]{3,2,1,0:T(8,128)(2,1)}, u32[]{:S(2)}) copy-start(bf16[1,1,720,1536]{3,2,1,0:T(8,128)(2,1)} %param.5) | copy-start | bytes 6635524
  1.6 1.1 copy-start.1
  2.7 0.7 copy-start.2

commit v3 on v2

--- a/solution.py
+++ b/solution.py
@@ -183,16 +183,28 @@
             src_ref=src, dst_ref=dst, send_sem=sem.at[k, step], recv_sem=land_sem.at[k, source],
             device_id=(leaf, row + way), device_id_type=MESH)
 
+    flying = {}
+
+    def hop_begin(way, can, make):
+        if way in flying:
+            before, earlier = flying[way]
+
+            @pl.when(before)
+            def _():
+                earlier().wait_send()
+
+        @pl.when(can)
+        def _():
+            make().start()
+
+        flying[way] = (can, make)
+
     def gather_start(name, slot, src=None):
         for way, can in ((1, row < rows_n - 1), (-1, row > 0)):
             def make(way=way):
                 return hop(name, slot(row) if src is None else src, slot(row), 0, row, way)
 
-            @pl.when(can)
-            def _(make=make):
-                make().start()
-
-            pending.append((can, make))
+            hop_begin(way, can, make)
 
     def gather_step(name, slot, step):
         for way, can in ((1, row < rows_n - 1), (-1, row > 0)):
@@ -207,13 +219,7 @@
                 make().wait_recv()
 
             if step < rows_n - 1:
-                both = jnp.logical_and(there, can)
-
-                @pl.when(both)
-                def _(make=make):
-                    make().start()
-
-                pending.append((both, make))
+                hop_begin(way, jnp.logical_and(there, can), make)
 
     def direct(name, slot, e):
         k = GATHERS.index(name)
@@ -291,7 +297,7 @@
     fixed.append(("d2", 2, lambda target: inv.at[level_rows(2)], lambda sender, d: d2.at[sender]))
     fixed.append(("b3", 3, lambda target: rhs.at[level_rows(3), at_cols(block_of(target))], lambda sender, d: b3.at[sender]))
     fixed.append(("d3", 3, lambda target: inv.at[level_rows(3)], lambda sender, d: d3.at[sender]))
-    for entry in fixed:
+    for entry in fixed[: CHUNKS + 1]:
         swap_start(*entry)
 
     def live(pair):
@@ -312,6 +318,8 @@
         y0[c, row] = solved.astype(jnp.bfloat16)
         gather_start("y0" + suffix[c], y0_slot(c))
         out[pl.ds(0, height), cols_of(c)] = solved
+    for entry in fixed[CHUNKS + 1 :]:
+        swap_start(*entry)
     for step in range(1, rows_n - 1):
         for c in range(CHUNKS):
             gather_step("y0" + suffix[c], y0_slot(c), step)
@@ -524,6 +532,7 @@
         out[level_rows(3), pl.ds(k * wide, wide)] = jnp.where(
             low_out, y3r[first].astype(jnp.float32), y3r[first + leaves_n // 2].astype(jnp.float32))
 
+    pending.extend(flying.values())
     for can, make in pending:
         if can is None:
             make().wait_send()
@@ -594,7 +603,7 @@
         out_specs=pl.BlockSpec(memory_space=pltpu.VMEM),
         scratch_shapes=scratch,
         compiler_params=pltpu.CompilerParams(
-            collective_id=0, has_side_effects=True, vmem_limit_bytes=48 * 2**20),
+            collective_id=0, has_side_effects=True, vmem_limit_bytes=63 * 2**20),
         cost_estimate=pl.CostEstimate(flops=flops, bytes_accessed=moved, transcendentals=0),
     )(pair_mask[0, 0], rhs[0, 0], inv_diag[0, 0], off_diag[0, 0])
     return solved[None, None]

time: 132 us -> 139 us (1.053)
  Pallas kernels: 127 us -> 136 us
  local copies, waits for them, and re-layouts: 4.51 us -> 2.59 us
    pallas_call x1, Pallas kernels: 127 us -> 136 us  [tree_shards(): pl.pallas_call(functools.partial(tree_kernel, rows_n, leaves_n), out_shap...]
    unnamed x7 -> x1, local copies, waits for them, and re-layouts: 4.51 us -> 2.59 us
where the time goes in v3:
time: 139 us; the launch traced here: 138 us
  Pallas kernels  136 us (98%)
  local copies, waits for them, and re-layouts  2.59 us (2%)
    pallas_call x1, Pallas kernels, tree_shards(): pl.pallas_call(functools.partial(tree_kernel, rows_n, leaves_n), out_shap...  136 us

profile of v3, /device:TPU:0, one launch (start us, length us, event | category | flops | bytes accessed | tf_op | source)
XLA Modules:
  0.0 138.4 jit_solution(15038638125107153882)
XLA Ops:
  0.0 135.8 %shard_map.46 = f32[720,512]{1,0:T(8,128)} custom-call(s32[6]{0:T(128)} %bitcast.9, bf16[720,512]{1,0:T(8,128)(2,1)} %bitcast.8, bf16[720,1536]{1,0:T(8,128)(2,1)} %bitcast.7, bf16[384,6528]{1,0:T(8,128)(2,1)} %bitcast.6), custom_call_target="tpu_custom_call" | custom-call | flops 3699376128 | bytes 9437184 | tf_op jit(solution)/shard_map/pallas_call | solution.py:599
  135.8 2.6 %copy.6 = f32[1,1,720,512]{3,2,1,0:T(8,128)} copy(f32[1,1,720,512]{3,2,1,0:T(8,128)} %bitcast.5) | data formatting | bytes 2949120

commit v4 on v2

--- a/solution.py
+++ b/solution.py
@@ -100,7 +100,7 @@
 
 
 GATHERS = ["z0a", "z0b", "y0a", "y0b", "z1a", "z1b", "y1a", "y1b", "z2", "z3"]
-SWAPS = ["b1a", "b1b", "b2", "b3", "d1", "d2", "d3", "u1a", "u1b", "u2", "u3", "y1a", "y1b", "y3"]
+SWAPS = ["b1a", "b1b", "b2", "b3", "d1", "d2", "d3", "d2p", "d3p", "u1a", "u1b", "u2", "u3", "y1a", "y1b", "y3"]
 LOCALS = ["z0a", "z0b", "d0", "p1", "p2", "p3", "d1", "d2", "d3", "b1a", "b1b", "b2", "b3"]
 
 
@@ -176,17 +176,25 @@
                 make().start()
         pending.append((can, make))
 
-    def hop(name, src, dst, step, source, way):
+    def hop(name, src, dst, step, source, order, way):
         k = GATHERS.index(name)
-        sem = up_sem if way > 0 else down_sem
+        sem = (up_sem, down_sem)[order]
         return pltpu.make_async_remote_copy(
             src_ref=src, dst_ref=dst, send_sem=sem.at[k, step], recv_sem=land_sem.at[k, source],
             device_id=(leaf, row + way), device_id_type=MESH)
 
+    lead = 1 - 2 * (leaf % 2)
+    ways = [(order, lead if order == 0 else -lead) for order in range(2)]
+
+    def inside(index):
+        return jnp.logical_and(index >= 0, index < rows_n)
+
     def gather_start(name, slot, src=None):
-        for way, can in ((1, row < rows_n - 1), (-1, row > 0)):
-            def make(way=way):
-                return hop(name, slot(row) if src is None else src, slot(row), 0, row, way)
+        for order, way in ways:
+            can = inside(row + way)
+
+            def make(order=order, way=way):
+                return hop(name, slot(row) if src is None else src, slot(row), 0, row, order, way)
 
             @pl.when(can)
             def _(make=make):
@@ -195,12 +203,13 @@
             pending.append((can, make))
 
     def gather_step(name, slot, step):
-        for way, can in ((1, row < rows_n - 1), (-1, row > 0)):
+        for order, way in ways:
+            can = inside(row + way)
             source = row - way * step
-            there = (source >= 0) if way > 0 else (source < rows_n)
-
-            def make(way=way, source=source):
-                return hop(name, slot(source), slot(source), step, source, way)
+            there = inside(source)
+
+            def make(order=order, way=way, source=source):
+                return hop(name, slot(source), slot(source), step, source, order, way)
 
             @pl.when(there)
             def _(make=make):
@@ -237,15 +246,16 @@
         size = 2**m
         return leaf - place[m] + (place[m] + d) % size
 
-    def swap(name, m, d, src, dst):
+    def swap(name, m, d, src, dst, line=None):
         k = SWAPS.index(name)
+        line = d if line is None else line
         return pltpu.make_async_remote_copy(
-            src_ref=src, dst_ref=dst, send_sem=swap_send.at[k, d], recv_sem=swap_recv.at[k, d],
+            src_ref=src, dst_ref=dst, send_sem=swap_send.at[k, line], recv_sem=swap_recv.at[k, line],
             device_id=(peer(m, d), row), device_id_type=MESH)
 
-    def swap_start(name, m, src, dst, when=None):
+    def swap_start(name, m, src, dst, when=None, only=None):
         size = 2**m
-        for d in range(1, size):
+        for d in only or range(1, size):
             target = (place[m] + d) % size
 
             def make(d=d, target=target):
@@ -253,9 +263,9 @@
 
             begin(None if when is None else when(target), make)
 
-    def swap_wait(name, m, src, dst):
+    def swap_wait(name, m, src, dst, only=None):
         size = 2**m
-        for d in range(1, size):
+        for d in only or range(1, size):
             sender = (place[m] - d + size) % size
             swap(name, m, d, src(place[m]), dst(sender, d)).wait_recv()
 
@@ -291,8 +301,22 @@
     fixed.append(("d2", 2, lambda target: inv.at[level_rows(2)], lambda sender, d: d2.at[sender]))
     fixed.append(("b3", 3, lambda target: rhs.at[level_rows(3), at_cols(block_of(target))], lambda sender, d: b3.at[sender]))
     fixed.append(("d3", 3, lambda target: inv.at[level_rows(3)], lambda sender, d: d3.at[sender]))
-    for entry in fixed:
-        swap_start(*entry)
+    D2, D3 = CHUNKS + 2, CHUNKS + 4
+    for k, entry in enumerate(fixed):
+        if k not in (D2, D3):
+            swap_start(*entry)
+
+    def hand_over(name, held, i, mine):
+        at = 2 * i + (place[1] if mine else 1 - place[1])
+        return swap(name, 1, 1, held.at[at], held.at[at], i)
+
+    def hand_all(name, held):
+        for i in range(held.shape[0] // 2):
+            begin(None, lambda i=i: hand_over(name, held, i, True))
+
+    def taken_all(name, held):
+        for i in range(held.shape[0] // 2):
+            hand_over(name, held, i, False).wait_recv()
 
     def live(pair):
         return mask[pair].astype(jnp.float32)
@@ -300,9 +324,15 @@
     def cols_of(c):
         return pl.ds(c * chunk, chunk)
 
+    pieces = [(D2, 2), (D3, 2), (D3, 4), (D3, 6)]
     for step in range(1, rows_n - 1):
         for c in range(CHUNKS):
             gather_step("z0" + suffix[c], z0_slot(c), step)
+            if pieces:
+                entry, d = pieces.pop(0)
+                swap_start(*fixed[entry], only=[d])
+    for entry, d in pieces:
+        swap_start(*fixed[entry], only=[d])
     local_copies["d0"].wait()
     whole = d0.shape[1]
     for c in range(CHUNKS):
@@ -315,8 +345,12 @@
     for step in range(1, rows_n - 1):
         for c in range(CHUNKS):
             gather_step("y0" + suffix[c], y0_slot(c), step)
-    for name in ("p1", "p2", "p3"):
+    for name in ("p1", "p2", "p3", "d2", "d3"):
         local_copies[name].wait()
+    swap_wait(*fixed[D2], only=[2])
+    swap_wait(*fixed[D3], only=[2, 4, 6])
+    hand_all("d2p", d2)
+    hand_all("d3p", d3)
 
     half = whole // 2
     u1_src = [lambda target, c=c: u1s.at[c, :, at_cols(target)] for c in range(CHUNKS)]
@@ -499,16 +533,14 @@
     later_3(0)
     reduce_2(0)
     update_2(1)
-    local_copies["d2"].wait()
-    swap_wait(*fixed[CHUNKS + 2])
+    taken_all("d2p", d2)
     reduce_2(1)
     later_3(1)
     for c in range(CHUNKS):
         out[level_rows(1), cols_of(c)] = y1[c, row].astype(jnp.float32)
     local_copies["b3"].wait()
     swap_wait(*fixed[CHUNKS + 3])
-    local_copies["d3"].wait()
-    swap_wait(*fixed[CHUNKS + 4])
+    taken_all("d3p", d3)
     solve_2(0)
     solve_2(1)
     update_3(0)
@@ -594,7 +626,7 @@
         out_specs=pl.BlockSpec(memory_space=pltpu.VMEM),
         scratch_shapes=scratch,
         compiler_params=pltpu.CompilerParams(
-            collective_id=0, has_side_effects=True, vmem_limit_bytes=48 * 2**20),
+            collective_id=0, has_side_effects=True, vmem_limit_bytes=125 * 2**19),
         cost_estimate=pl.CostEstimate(flops=flops, bytes_accessed=moved, transcendentals=0),
     )(pair_mask[0, 0], rhs[0, 0], inv_diag[0, 0], off_diag[0, 0])
     return solved[None, None]

time: 132 us -> 131 us (level)
  local copies, waits for them, and re-layouts: 4.51 us -> 2.59 us
    unnamed x7 -> x1, local copies, waits for them, and re-layouts: 4.51 us -> 2.59 us
where the time goes in v4:
time: 131 us
  Pallas kernels  128 us (98%)
  local copies, waits for them, and re-layouts  2.59 us (2%)
    pallas_call x1, Pallas kernels, tree_shards(): pl.pallas_call(functools.partial(tree_kernel, rows_n, leaves_n), out_shap...  128 us

profile of v4, /device:TPU:0, one launch (start us, length us, event | category | flops | bytes accessed | tf_op | source)
XLA Modules:
  0.0 130.7 jit_solution(16079221975852449712)
XLA Ops:
  0.0 128.1 %shard_map.46 = f32[720,512]{1,0:T(8,128)} custom-call(s32[6]{0:T(128)} %bitcast.9, bf16[720,512]{1,0:T(8,128)(2,1)} %bitcast.8, bf16[720,1536]{1,0:T(8,128)(2,1)} %bitcast.7, bf16[384,6528]{1,0:T(8,128)(2,1)} %bitcast.6), custom_call_target="tpu_custom_call" | custom-call | flops 3699376128 | bytes 9437184 | tf_op jit(solution)/shard_map/pallas_call | solution.py:622
  128.1 2.6 %copy.6 = f32[1,1,720,512]{3,2,1,0:T(8,128)} copy(f32[1,1,720,512]{3,2,1,0:T(8,128)} %bitcast.5) | data formatting | bytes 2949120

commit v5 on v4

--- a/solution.py
+++ b/solution.py
@@ -109,7 +109,7 @@
     mask, rhs, inv, pan, out,
     d0, d1, d2, d3, p1, p2, p3, b1, b2, b3,
     z0, z1, z2, z3, y0, y1, y2,
-    u1, u2, u3, u1s, u2s, u3s, u1r, u2r, u3r, y1s, y2s, y3s, y3r,
+    acc, u1, u2, u3, u1s, u2s, u3s, u1r, u2r, u3r, y1s, y2s, y3s, y3r,
     up_sem, down_sem, land_sem, swap_send, swap_recv, local_sem, spread_send, spread_recv,
 ):
     leaf = lax.axis_index("leaf")
@@ -202,7 +202,15 @@
 
             pending.append((can, make))
 
-    def gather_step(name, slot, step):
+    def arrived(step, then):
+        for _, way in ways:
+            source = row - way * step
+
+            @pl.when(inside(source))
+            def _(source=source):
+                then(source)
+
+    def gather_step(name, slot, step, then=None):
         for order, way in ways:
             can = inside(row + way)
             source = row - way * step
@@ -223,6 +231,9 @@
                     make().start()
 
                 pending.append((both, make))
+
+        if then is not None:
+            arrived(step, then)
 
     def direct(name, slot, e):
         k = GATHERS.index(name)
@@ -324,33 +335,69 @@
     def cols_of(c):
         return pl.ds(c * chunk, chunk)
 
+    whole = d0.shape[1]
+
+    def shard_cols(source):
+        return pl.ds(pl.multiple_of(source * height, LANES), height)
+
+    def add_solved(c):
+        def then(source):
+            acc[c] += dot32(d0[:, shard_cols(source)], z0[c, source])
+        return then
+
+    def add_first(c):
+        def then(source):
+            u1[c] += dot32(p1[:, shard_cols(source)], y0[c, source]) * live(0)
+        return then
+
+    def add_rest(c):
+        def then(source):
+            u2[:, cols_of(c)] += dot32(p2[:, shard_cols(source)], y0[c, source]) * live(1)
+            u3[:, cols_of(c)] += dot32(p3[:, shard_cols(source)], y0[c, source]) * live(3)
+        return then
+
+    def add_all(c):
+        def then(source):
+            add_first(c)(source)
+            add_rest(c)(source)
+        return then
+
+    for c in range(CHUNKS):
+        acc[c] = jnp.zeros_like(acc[c])
+        u1[c] = jnp.zeros_like(u1[c])
+    u2[...] = jnp.zeros_like(u2)
+    u3[...] = jnp.zeros_like(u3)
+    local_copies["d0"].wait()
+    for c in range(CHUNKS):
+        local_copies["z0" + suffix[c]].wait()
+        add_solved(c)(row)
     pieces = [(D2, 2), (D3, 2), (D3, 4), (D3, 6)]
     for step in range(1, rows_n - 1):
         for c in range(CHUNKS):
-            gather_step("z0" + suffix[c], z0_slot(c), step)
+            gather_step("z0" + suffix[c], z0_slot(c), step, add_solved(c))
             if pieces:
                 entry, d = pieces.pop(0)
                 swap_start(*fixed[entry], only=[d])
     for entry, d in pieces:
         swap_start(*fixed[entry], only=[d])
-    local_copies["d0"].wait()
-    whole = d0.shape[1]
-    for c in range(CHUNKS):
-        local_copies["z0" + suffix[c]].wait()
-        gather_step("z0" + suffix[c], z0_slot(c), rows_n - 1)
-        solved = dot32(d0[...], z0[c].reshape(whole, chunk))
+    for c in range(CHUNKS):
+        gather_step("z0" + suffix[c], z0_slot(c), rows_n - 1, add_solved(c))
+        solved = acc[c]
         y0[c, row] = solved.astype(jnp.bfloat16)
         gather_start("y0" + suffix[c], y0_slot(c))
         out[pl.ds(0, height), cols_of(c)] = solved
+    for name in ("p1", "p2", "p3", "d2", "d3"):
+        local_copies[name].wait()
+    for c in range(CHUNKS):
+        add_all(c)(row)
     for step in range(1, rows_n - 1):
         for c in range(CHUNKS):
-            gather_step("y0" + suffix[c], y0_slot(c), step)
-    for name in ("p1", "p2", "p3", "d2", "d3"):
-        local_copies[name].wait()
-    swap_wait(*fixed[D2], only=[2])
-    swap_wait(*fixed[D3], only=[2, 4, 6])
-    hand_all("d2p", d2)
-    hand_all("d3p", d3)
+            gather_step("y0" + suffix[c], y0_slot(c), step, add_all(c))
+        if step == 1:
+            swap_wait(*fixed[D2], only=[2])
+            swap_wait(*fixed[D3], only=[2, 4, 6])
+            hand_all("d2p", d2)
+            hand_all("d3p", d3)
 
     half = whole // 2
     u1_src = [lambda target, c=c: u1s.at[c, :, at_cols(target)] for c in range(CHUNKS)]
@@ -359,10 +406,8 @@
     y1_dst = [lambda sender, d, c=c: y1.at[c, row, :, at_cols(sender)] for c in range(CHUNKS)]
 
     def update_1(c):
-        gather_step("y0" + suffix[c], y0_slot(c), rows_n - 1)
-        update = dot32(p1[...], y0[c].reshape(whole, chunk)) * live(0)
-        u1[c] = update
-        u1s[c] = update.astype(jnp.bfloat16)
+        gather_step("y0" + suffix[c], y0_slot(c), rows_n - 1, add_first(c))
+        u1s[c] = u1[c].astype(jnp.bfloat16)
         swap_start("u1" + suffix[c], 1, u1_src[c], u1_dst[c])
 
     def reduce_1(c):
@@ -374,12 +419,6 @@
         for s in range(2):
             z1[c, s, row] = reduced[s * heights[1] : (s + 1) * heights[1]]
         gather_start("z1" + suffix[c], z1_slot(c))
-
-    def early_2(c):
-        u2[:, cols_of(c)] = dot32(p2[:, :whole], y0[c].reshape(whole, chunk)) * live(1)
-
-    def early_3(c):
-        u3[:, cols_of(c)] = dot32(p3[:, :whole], y0[c].reshape(whole, chunk)) * live(3)
 
     def solve_1(c):
         gather_step("z1" + suffix[c], z1_slot(c), rows_n - 1)
@@ -504,14 +543,12 @@
         y3r[place[3]] = y3s[place[3]]
 
     update_1(0)
-    early_2(0)
+    arrived(rows_n - 1, add_rest(0))
     reduce_1(0)
-    early_3(0)
     update_1(1)
     gather_step("z1a", z1_slot(0), 1)
     reduce_1(1)
-    early_2(1)
-    early_3(1)
+    arrived(rows_n - 1, add_rest(1))
     for step in range(2, rows_n - 1):
         gather_step("z1a", z1_slot(0), step)
         gather_step("z1b", z1_slot(1), step - 1)
@@ -572,6 +609,7 @@
         leaves_n == 2**TREE_LEVELS
         and rows_n > 2
         and whole % (leaves_n * rows_n * ROW_TILE) == 0
+        and whole % (rows_n * LANES) == 0
         and whole % (4 * LANES) == 0
         and right_n == 4 * LANES
     )
@@ -600,6 +638,7 @@
         vm((CHUNKS, rows_n, height, chunk), bf16),
         vm((CHUNKS, rows_n, hs[1], chunk), bf16),
         vm((rows_n, hs[2], right_n), bf16),
+        vm((CHUNKS, height, chunk), f32),
         vm((CHUNKS, height, chunk), f32), vm((height, right_n), f32), vm((height, right_n), f32),
         vm((CHUNKS, height, chunk), bf16), vm((height, right_n), bf16),
         vm((leaves_n, height // 2, LANES), bf16),
@@ -626,7 +665,7 @@
         out_specs=pl.BlockSpec(memory_space=pltpu.VMEM),
         scratch_shapes=scratch,
         compiler_params=pltpu.CompilerParams(
-            collective_id=0, has_side_effects=True, vmem_limit_bytes=125 * 2**19),
+            collective_id=0, has_side_effects=True, vmem_limit_bytes=62 * 2**20),
         cost_estimate=pl.CostEstimate(flops=flops, bytes_accessed=moved, transcendentals=0),
     )(pair_mask[0, 0], rhs[0, 0], inv_diag[0, 0], off_diag[0, 0])
     return solved[None, None]

time: 131 us -> 129 us (0.985)
    pallas_call x1, Pallas kernels: 128 us -> 127 us  [tree_shards(): pl.pallas_call(functools.partial(tree_kernel, rows_n, leaves_n), out_shap...]
where the time goes in v5:
time: 129 us
  Pallas kernels  127 us (98%)
  local copies, waits for them, and re-layouts  2.59 us (2%)
    pallas_call x1, Pallas kernels, tree_shards(): pl.pallas_call(functools.partial(tree_kernel, rows_n, leaves_n), out_shap...  127 us
    unnamed x1, local copies, waits for them, and re-layouts  2.59 us

profile of v5, /device:TPU:0, one launch (start us, length us, event | category | flops | bytes accessed | tf_op | source)
XLA Modules:
  0.0 129.2 jit_solution(12211645977499682740)
XLA Ops:
  0.0 126.6 %shard_map.46 = f32[720,512]{1,0:T(8,128)} custom-call(s32[6]{0:T(128)} %bitcast.9, bf16[720,512]{1,0:T(8,128)(2,1)} %bitcast.8, bf16[720,1536]{1,0:T(8,128)(2,1)} %bitcast.7, bf16[384,6528]{1,0:T(8,128)(2,1)} %bitcast.6), custom_call_target="tpu_custom_call" | custom-call | flops 3699376128 | bytes 9437184 | tf_op jit(solution)/shard_map/pallas_call | solution.py:661
  126.6 2.6 %copy.6 = f32[1,1,720,512]{3,2,1,0:T(8,128)} copy(f32[1,1,720,512]{3,2,1,0:T(8,128)} %bitcast.5) | data formatting | bytes 2949120

commit v6 on v5

--- a/solution.py
+++ b/solution.py
@@ -12,6 +12,7 @@
 CHUNKS = 2
 TREE_LEVELS = 3
 MESH = pl.DeviceIdType.MESH
+REACH = 2
 
 
 def partner_2(block, axis, bit):
@@ -176,12 +177,12 @@
                 make().start()
         pending.append((can, make))
 
-    def hop(name, src, dst, step, source, order, way):
+    def hop(name, src, dst, step, source, order, way, far=1):
         k = GATHERS.index(name)
         sem = (up_sem, down_sem)[order]
         return pltpu.make_async_remote_copy(
             src_ref=src, dst_ref=dst, send_sem=sem.at[k, step], recv_sem=land_sem.at[k, source],
-            device_id=(leaf, row + way), device_id_type=MESH)
+            device_id=(leaf, row + way * far), device_id_type=MESH)
 
     lead = 1 - 2 * (leaf % 2)
     ways = [(order, lead if order == 0 else -lead) for order in range(2)]
@@ -190,17 +191,13 @@
         return jnp.logical_and(index >= 0, index < rows_n)
 
     def gather_start(name, slot, src=None):
-        for order, way in ways:
-            can = inside(row + way)
-
-            def make(order=order, way=way):
-                return hop(name, slot(row) if src is None else src, slot(row), 0, row, order, way)
-
-            @pl.when(can)
-            def _(make=make):
-                make().start()
-
-            pending.append((can, make))
+        for far, (order, way) in [(far, pair) for far in reversed(range(1, REACH + 1)) for pair in ways]:
+            can = inside(row + way * far)
+
+            def make(order=order, way=way, far=far):
+                return hop(name, slot(row) if src is None else src, slot(row), far - 1, row, order, way, far)
+
+            begin(can, make)
 
     def arrived(step, then):
         for _, way in ways:
@@ -223,7 +220,7 @@
             def _(make=make):
                 make().wait_recv()
 
-            if step < rows_n - 1:
+            if REACH <= step < rows_n - 1:
                 both = jnp.logical_and(there, can)
 
                 @pl.when(both)
@@ -385,7 +382,7 @@
         solved = acc[c]
         y0[c, row] = solved.astype(jnp.bfloat16)
         gather_start("y0" + suffix[c], y0_slot(c))
-        out[pl.ds(0, height), cols_of(c)] = solved
+        out[pl.ds(0, height), cols_of(c)] = y0[c, row]
     for name in ("p1", "p2", "p3", "d2", "d3"):
         local_copies[name].wait()
     for c in range(CHUNKS):
@@ -574,7 +571,7 @@
     reduce_2(1)
     later_3(1)
     for c in range(CHUNKS):
-        out[level_rows(1), cols_of(c)] = y1[c, row].astype(jnp.float32)
+        out[level_rows(1), cols_of(c)] = y1[c, row]
     local_copies["b3"].wait()
     swap_wait(*fixed[CHUNKS + 3])
     taken_all("d3p", d3)
@@ -584,14 +581,15 @@
     reduce_3(0)
     update_3(1)
     reduce_3(1)
-    out[level_rows(2), :] = y2[row].astype(jnp.float32)
+    out[level_rows(2), :] = y2[row]
     solve_3()
     swap_wait("y3", 3, y3_src, y3_dst)
     low_out = lax.broadcasted_iota(jnp.int32, (heights[3], wide), 1) < wide // 2
     for k in range(leaves_n // 2):
         first = 2 * (k % 2) + k // 2
         out[level_rows(3), pl.ds(k * wide, wide)] = jnp.where(
-            low_out, y3r[first].astype(jnp.float32), y3r[first + leaves_n // 2].astype(jnp.float32))
+            low_out, y3r[first].astype(jnp.float32), y3r[first + leaves_n // 2].astype(jnp.float32)
+        ).astype(jnp.bfloat16)
 
     for can, make in pending:
         if can is None:
@@ -660,7 +658,7 @@
     moved = 2 * (pack * whole + height * off_diag.shape[3] + 3 * pack * right_n)
     solved = pl.pallas_call(
         functools.partial(tree_kernel, rows_n, leaves_n),
-        out_shape=jax.ShapeDtypeStruct((pack, right_n), f32),
+        out_shape=jax.ShapeDtypeStruct((pack, right_n), bf16),
         in_specs=[pl.BlockSpec(memory_space=pltpu.SMEM)] + [pl.BlockSpec(memory_space=pltpu.HBM)] * 3,
         out_specs=pl.BlockSpec(memory_space=pltpu.VMEM),
         scratch_shapes=scratch,
@@ -668,7 +666,7 @@
             collective_id=0, has_side_effects=True, vmem_limit_bytes=62 * 2**20),
         cost_estimate=pl.CostEstimate(flops=flops, bytes_accessed=moved, transcendentals=0),
     )(pair_mask[0, 0], rhs[0, 0], inv_diag[0, 0], off_diag[0, 0])
-    return solved[None, None]
+    return solved.astype(f32)[None, None]
 
 
 def solution(mesh):

time: 129 us -> 152 us (1.18)
  Pallas kernels: 127 us -> 150 us
  local copies, waits for them, and re-layouts: 2.59 us -> 0 us
  other arithmetic: 0 us -> 2.43 us
    pallas_call x1, Pallas kernels: 127 us -> 150 us  [tree_shards(): pl.pallas_call(functools.partial(tree_kernel, rows_n, leaves_n), out_shap...]
    unnamed x1 -> x0, local copies, waits for them, and re-layouts: 2.59 us -> none
    broadcast_in_dim x0 -> x1, other arithmetic: none -> 2.43 us  [tree_shards(): return solved.astype(f32)[None, None]]
where the time goes in v6:
time: 152 us
  Pallas kernels  150 us (99%)
  other arithmetic  2.43 us (2%)
    pallas_call x1, Pallas kernels, tree_shards(): pl.pallas_call(functools.partial(tree_kernel, rows_n, leaves_n), out_shap...  150 us

profile of v6, /device:TPU:0, one launch (start us, length us, event | category | flops | bytes accessed | tf_op | source)
XLA Modules:
  0.0 152.0 jit_solution(1915918937248579278)
XLA Ops:
  0.0 149.5 %shard_map.46 = bf16[720,512]{1,0:T(8,128)(2,1)} custom-call(s32[6]{0:T(128)} %bitcast.10, bf16[720,512]{1,0:T(8,128)(2,1)} %bitcast.9, bf16[720,1536]{1,0:T(8,128)(2,1)} %bitcast.8, bf16[384,6528]{1,0:T(8,128)(2,1)} %bitcast.7), custom_call_target="tpu_custom_call" | custom-call | flops 3699376128 | bytes 9437184 | tf_op jit(solution)/shard_map/pallas_call | solution.py:659
  149.5 2.4 %bitcast_convert_fusion = f32[1,1,720,512]{3,2,1,0:T(8,128)} fusion(bf16[720,512]{1,0:T(8,128)(2,1)} %shard_map.46), kind=kLoop, calls=%fused_computation | loop fusion | flops 368640 | bytes 2211840 | tf_op jit(solution)/shard_map/broadcast_in_dim | solution.py:669

commit v7 on v6

--- a/solution.py
+++ b/solution.py
@@ -12,7 +12,7 @@
 CHUNKS = 2
 TREE_LEVELS = 3
 MESH = pl.DeviceIdType.MESH
-REACH = 2
+REACH = 1
 
 
 def partner_2(block, axis, bit):
@@ -190,9 +190,9 @@
     def inside(index):
         return jnp.logical_and(index >= 0, index < rows_n)
 
-    def gather_start(name, slot, src=None):
+    def gather_start(name, slot, src=None, gate=True):
         for far, (order, way) in [(far, pair) for far in reversed(range(1, REACH + 1)) for pair in ways]:
-            can = inside(row + way * far)
+            can = jnp.logical_and(inside(row + way * far), gate)
 
             def make(order=order, way=way, far=far):
                 return hop(name, slot(row) if src is None else src, slot(row), far - 1, row, order, way, far)
@@ -207,11 +207,11 @@
             def _(source=source):
                 then(source)
 
-    def gather_step(name, slot, step, then=None):
+    def gather_step(name, slot, step, then=None, gate=True):
         for order, way in ways:
             can = inside(row + way)
             source = row - way * step
-            there = inside(source)
+            there = jnp.logical_and(inside(source), gate)
 
             def make(order=order, way=way, source=source):
                 return hop(name, slot(source), slot(source), step, source, order, way)
@@ -231,24 +231,6 @@
 
         if then is not None:
             arrived(step, then)
-
-    def direct(name, slot, e):
-        k = GATHERS.index(name)
-        return pltpu.make_async_remote_copy(
-            src_ref=slot(row), dst_ref=slot(row), send_sem=up_sem.at[k, e], recv_sem=land_sem.at[k, e],
-            device_id=(leaf, (row + e) % rows_n), device_id_type=MESH)
-
-    def direct_start(name, slot, can):
-        for e in range(1, rows_n):
-            begin(can, lambda e=e: direct(name, slot, e))
-
-    def direct_wait(name, slot):
-        k = GATHERS.index(name)
-        for e in range(1, rows_n):
-            there = slot((row - e + rows_n) % rows_n)
-            pltpu.make_async_remote_copy(
-                src_ref=there, dst_ref=there, send_sem=up_sem.at[k, e], recv_sem=land_sem.at[k, e],
-                device_id=(leaf, (row + e) % rows_n), device_id_type=MESH).wait_recv()
 
     def peer(m, d):
         size = 2**m
@@ -452,7 +434,7 @@
             for s in range(4):
                 z2[s, row] = reduced[s * heights[2] : (s + 1) * heights[2]]
 
-        direct_start("z2", z2_slot, own_chunk == c)
+        gather_start("z2", z2_slot, gate=own_chunk == c)
 
     def spread(d, e, position):
         here = leaf - place[2] + (place[2] + d) % 4
@@ -466,9 +448,10 @@
     others = [(d, e) for e in reversed(range(rows_n)) for d in range(4) if d or e]
 
     def solve_2(c):
+        gather_step("z2", z2_slot, rows_n - 1, gate=own_chunk == c)
+
         @pl.when(own_chunk == c)
         def _():
-            direct_wait("z2", z2_slot)
             solved = dot32(d2[...].reshape(height, whole), z2[...].reshape(whole, wide)).astype(jnp.bfloat16)
             y2s[...] = solved.reshape(4, heights[2], wide)
 
@@ -522,13 +505,13 @@
             for s in range(4):
                 z3[s, row] = reduced[s * heights[3] : (s + 1) * heights[3]]
 
-        direct_start("z3", z3_slot, own_chunk == c)
+        gather_start("z3", z3_slot, gate=own_chunk == c)
 
     y3_src = lambda target: y3s.at[target]
     y3_dst = lambda sender, d: y3r.at[sender]
 
     def solve_3():
-        direct_wait("z3", z3_slot)
+        gather_step("z3", z3_slot, rows_n - 1)
         known = z3[...].reshape(half, wide)
         left = dot32(d3[:, :, :half].reshape(height, half), known)
         right = dot32(d3[:, :, half:].reshape(height, half), known)
@@ -566,10 +549,15 @@
     gather_step("y1b", y1_slot(1), rows_n - 2)
     later_3(0)
     reduce_2(0)
+    gather_step("z2", z2_slot, 1, gate=own_chunk == 0)
     update_2(1)
+    for step in range(2, rows_n - 1):
+        gather_step("z2", z2_slot, step, gate=own_chunk == 0)
     taken_all("d2p", d2)
     reduce_2(1)
     later_3(1)
+    for step in range(1, rows_n - 1):
+        gather_step("z2", z2_slot, step, gate=own_chunk == 1)
     for c in range(CHUNKS):
         out[level_rows(1), cols_of(c)] = y1[c, row]
     local_copies["b3"].wait()
@@ -579,8 +567,13 @@
     solve_2(1)
     update_3(0)
     reduce_3(0)
+    gather_step("z3", z3_slot, 1, gate=own_chunk == 0)
     update_3(1)
+    for step in range(2, rows_n - 1):
+        gather_step("z3", z3_slot, step, gate=own_chunk == 0)
     reduce_3(1)
+    for step in range(1, rows_n - 1):
+        gather_step("z3", z3_slot, step, gate=own_chunk == 1)
     out[level_rows(2), :] = y2[row]
     solve_3()
     swap_wait("y3", 3, y3_src, y3_dst)

time: 152 us -> 136 us (0.89)
  Pallas kernels: 150 us -> 134 us
    pallas_call x1, Pallas kernels: 150 us -> 134 us  [tree_shards(): pl.pallas_call(functools.partial(tree_kernel, rows_n, leaves_n), out_shap...]
where the time goes in v7:
time: 136 us
  Pallas kernels  134 us (99%)
  other arithmetic  2.43 us (2%)
    pallas_call x1, Pallas kernels, tree_shards(): pl.pallas_call(functools.partial(tree_kernel, rows_n, leaves_n), out_shap...  134 us

profile of v7, /device:TPU:0, one launch (start us, length us, event | category | flops | bytes accessed | tf_op | source)
XLA Modules:
  0.0 136.2 jit_solution(18417954848665897117)
XLA Ops:
  0.0 133.8 %shard_map.46 = bf16[720,512]{1,0:T(8,128)(2,1)} custom-call(s32[6]{0:T(128)} %bitcast.10, bf16[720,512]{1,0:T(8,128)(2,1)} %bitcast.9, bf16[720,1536]{1,0:T(8,128)(2,1)} %bitcast.8, bf16[384,6528]{1,0:T(8,128)(2,1)} %bitcast.7), custom_call_target="tpu_custom_call" | custom-call | flops 3699376128 | bytes 9437184 | tf_op jit(solution)/shard_map/pallas_call | solution.py:652
  133.8 2.4 %bitcast_convert_fusion = f32[1,1,720,512]{3,2,1,0:T(8,128)} fusion(bf16[720,512]{1,0:T(8,128)(2,1)} %shard_map.46), kind=kLoop, calls=%fused_computation | loop fusion | flops 368640 | bytes 2211840 | tf_op jit(solution)/shard_map/broadcast_in_dim | solution.py:662

commit v8 on v5

--- a/solution.py
+++ b/solution.py
@@ -385,7 +385,7 @@
         solved = acc[c]
         y0[c, row] = solved.astype(jnp.bfloat16)
         gather_start("y0" + suffix[c], y0_slot(c))
-        out[pl.ds(0, height), cols_of(c)] = solved
+        out[pl.ds(0, height), cols_of(c)] = y0[c, row]
     for name in ("p1", "p2", "p3", "d2", "d3"):
         local_copies[name].wait()
     for c in range(CHUNKS):
@@ -548,10 +548,10 @@
     update_1(1)
     gather_step("z1a", z1_slot(0), 1)
     reduce_1(1)
-    arrived(rows_n - 1, add_rest(1))
     for step in range(2, rows_n - 1):
         gather_step("z1a", z1_slot(0), step)
         gather_step("z1b", z1_slot(1), step - 1)
+    arrived(rows_n - 1, add_rest(1))
     local_copies["d1"].wait()
     swap_wait(*fixed[CHUNKS])
     solve_1(0)
@@ -574,7 +574,7 @@
     reduce_2(1)
     later_3(1)
     for c in range(CHUNKS):
-        out[level_rows(1), cols_of(c)] = y1[c, row].astype(jnp.float32)
+        out[level_rows(1), cols_of(c)] = y1[c, row]
     local_copies["b3"].wait()
     swap_wait(*fixed[CHUNKS + 3])
     taken_all("d3p", d3)
@@ -584,14 +584,15 @@
     reduce_3(0)
     update_3(1)
     reduce_3(1)
-    out[level_rows(2), :] = y2[row].astype(jnp.float32)
+    out[level_rows(2), :] = y2[row]
     solve_3()
     swap_wait("y3", 3, y3_src, y3_dst)
     low_out = lax.broadcasted_iota(jnp.int32, (heights[3], wide), 1) < wide // 2
     for k in range(leaves_n // 2):
         first = 2 * (k % 2) + k // 2
         out[level_rows(3), pl.ds(k * wide, wide)] = jnp.where(
-            low_out, y3r[first].astype(jnp.float32), y3r[first + leaves_n // 2].astype(jnp.float32))
+            low_out, y3r[first].astype(jnp.float32), y3r[first + leaves_n // 2].astype(jnp.float32)
+        ).astype(jnp.bfloat16)
 
     for can, make in pending:
         if can is None:
@@ -660,7 +661,7 @@
     moved = 2 * (pack * whole + height * off_diag.shape[3] + 3 * pack * right_n)
     solved = pl.pallas_call(
         functools.partial(tree_kernel, rows_n, leaves_n),
-        out_shape=jax.ShapeDtypeStruct((pack, right_n), f32),
+        out_shape=jax.ShapeDtypeStruct((pack, right_n), bf16),
         in_specs=[pl.BlockSpec(memory_space=pltpu.SMEM)] + [pl.BlockSpec(memory_space=pltpu.HBM)] * 3,
         out_specs=pl.BlockSpec(memory_space=pltpu.VMEM),
         scratch_shapes=scratch,
@@ -668,7 +669,7 @@
             collective_id=0, has_side_effects=True, vmem_limit_bytes=62 * 2**20),
         cost_estimate=pl.CostEstimate(flops=flops, bytes_accessed=moved, transcendentals=0),
     )(pair_mask[0, 0], rhs[0, 0], inv_diag[0, 0], off_diag[0, 0])
-    return solved[None, None]
+    return solved.astype(f32)[None, None]
 
 
 def solution(mesh):

time: 129 us -> 129 us (level)
  local copies, waits for them, and re-layouts: 2.59 us -> 0 us
  other arithmetic: 0 us -> 2.43 us
    unnamed x1 -> x0, local copies, waits for them, and re-layouts: 2.59 us -> none
    broadcast_in_dim x0 -> x1, other arithmetic: none -> 2.43 us  [tree_shards(): return solved.astype(f32)[None, None]]
where the time goes in v8:
time: 129 us
  Pallas kernels  126 us (98%)
  other arithmetic  2.43 us (2%)
    pallas_call x1, Pallas kernels, tree_shards(): pl.pallas_call(functools.partial(tree_kernel, rows_n, leaves_n), out_shap...  126 us

profile of v8, /device:TPU:0, one launch (start us, length us, event | category | flops | bytes accessed | tf_op | source)
XLA Modules:
  0.0 128.8 jit_solution(6632458611314137521)
XLA Ops:
  0.0 126.4 %shard_map.46 = bf16[720,512]{1,0:T(8,128)(2,1)} custom-call(s32[6]{0:T(128)} %bitcast.10, bf16[720,512]{1,0:T(8,128)(2,1)} %bitcast.9, bf16[720,1536]{1,0:T(8,128)(2,1)} %bitcast.8, bf16[384,6528]{1,0:T(8,128)(2,1)} %bitcast.7), custom_call_target="tpu_custom_call" | custom-call | flops 3699376128 | bytes 9437184 | tf_op jit(solution)/shard_map/pallas_call | solution.py:662
  126.4 2.4 %bitcast_convert_fusion = f32[1,1,720,512]{3,2,1,0:T(8,128)} fusion(bf16[720,512]{1,0:T(8,128)(2,1)} %shard_map.46), kind=kLoop, calls=%fused_computation | loop fusion | flops 368640 | bytes 2211840 | tf_op jit(solution)/shard_map/broadcast_in_dim | solution.py:672
